TPU v7x, 256 devices: a whole 4x4x8 slice. The times are simulated.
256 devices in a mesh: dp: 4 (over x_hi, core), mx: 8 (over z), my: 8 (over x_lo, y).
Axes of the slice: x: 4 (x_hi: 2, x_lo: 2; x = x_hi * 2 + x_lo), y: 4, z: 8, core: 2. Of those that a mesh axis runs over, the one named last changes fastest.
Arguments:
- tokens: bfloat16 [8, 256, 6144], P(None, 'dp', ('mx', 'my')), may hold values from -170 to 170
- w_qkv: bfloat16 [6144, 3, 3072], P(('mx', 'dp'), None, 'my'), may hold values from -2 to 2
- w_up: bfloat16 [6144, 12288], P(('mx', 'dp'), 'my'), may hold values from -2 to 2
- w_proj: bfloat16 [3072, 6144], P('my', ('mx', 'dp')), may hold values from -0.109375 to 0.109375
- w_down: bfloat16 [12288, 6144], P('my', ('mx', 'dp')), may hold values from -0.0546875 to 0.0546875
- cotangent: bfloat16 [8, 256, 6144], P(None, 'dp', ('mx', 'my')), may hold values from -6 to 6
Outputs:
- update: bfloat16 [8, 256, 6144], P(None, 'dp', ('mx', 'my'))
- tokens_grad: bfloat16 [8, 256, 6144], P(None, 'dp', ('mx', 'my'))
- g_qkv: bfloat16 [6144, 3, 3072], P(('mx', 'dp'), None, 'my')
- g_up: bfloat16 [6144, 12288], P(('mx', 'dp'), 'my')
- g_proj: bfloat16 [3072, 6144], P('my', ('mx', 'dp'))
- g_down: bfloat16 [12288, 6144], P('my', ('mx', 'dp'))
All inputs are finite; a program needn't handle non-finite values.
Results may differ from a plain program's by a relative error of at most 0.034.
Values may be sent and summed in bfloat16 or wider, within the bound.
A program may use at most 64 MiB of HBM per device.

v0:
```python
import jax
import jax.numpy as jnp
from jax import lax
from jax.sharding import PartitionSpec as P

D = 6144
HD = 128
PATCHES = 256


EPS = 1e-06


def gelu_exact(values):
    return jax.nn.gelu(values, approximate=False)


def head_norm(head_block):
    average = jnp.mean(head_block, axis=-1, keepdims=True)
    centered = head_block - average
    inverse = lax.rsqrt(jnp.mean(centered * centered, axis=-1, keepdims=True) + EPS)
    return (centered * inverse, inverse)


def head_norm_back(upstream, normal, inverse):
    return inverse * (
        upstream
        - jnp.mean(upstream, axis=-1, keepdims=True)
        - normal * jnp.mean(upstream * normal, axis=-1, keepdims=True)
    )


def contract_rows(left_side, right_side):
    return lax.dot_general(
        left_side, right_side, (((0,), (0,)), ((), ())), preferred_element_type=jnp.float32
    )


def contract_cols(left_side, right_side):
    return lax.dot_general(
        left_side, right_side, (((1,), (1,)), ((), ())), preferred_element_type=jnp.float32
    )


def body(tokens, w_qkv, w_up, w_proj, w_down, cotangent):
    image_total, pat_loc, width_loc = tokens.shape
    tok_dp = image_total * pat_loc
    parts_mx = lax.axis_size("mx")
    img_loc = image_total // parts_mx
    tok_loc = img_loc * pat_loc
    local_rows = w_qkv.shape[0]
    per_head = w_qkv.shape[2]
    heads_loc = per_head // HD
    qkv_cols = 3 * per_head
    x_float = tokens.reshape(tok_dp, width_loc).astype(jnp.float32)
    totals = lax.psum(jnp.sum(x_float, axis=1), ("mx", "my"))
    centered = x_float - (totals / D)[:, None]
    spread = lax.psum(jnp.sum(centered * centered, axis=1), ("mx", "my"))
    variance = spread / D
    inverse = lax.rsqrt(variance + EPS)[:, None]
    standard = centered * inverse
    normed = standard.astype(jnp.bfloat16)
    features = lax.all_gather(normed, "my", axis=1, tiled=True)
    first_local = jnp.concatenate([w_qkv.reshape(local_rows, qkv_cols), w_up], axis=1)
    second_local = jnp.concatenate([w_proj, w_down], axis=0)
    col_block = features
    partial_in = jnp.dot(
        col_block,
        lax.all_gather(first_local, "dp", axis=0, tiled=True),
        preferred_element_type=jnp.float32,
    )
    branch_in = lax.psum_scatter(
        partial_in.astype(jnp.bfloat16), "mx", scatter_dimension=0, tiled=True
    ).astype(jnp.float32)
    projected = branch_in[:, :qkv_cols].reshape(tok_loc, 3, heads_loc, HD)
    query_hat, query_inv = head_norm(projected[:, 0])
    key_hat, key_inv = head_norm(projected[:, 1])
    query_low = query_hat.astype(jnp.bfloat16)
    key_low = key_hat.astype(jnp.bfloat16)
    value_low = projected[:, 2].astype(jnp.bfloat16)
    kv_local = jnp.concatenate(
        [key_low.reshape(tok_loc, per_head), value_low.reshape(tok_loc, per_head)], axis=1
    ).reshape(img_loc, pat_loc, 2 * per_head)
    kv_all = lax.all_gather(kv_local, "dp", axis=1, tiled=True)
    kv_image = kv_all.reshape(img_loc, PATCHES, 2, heads_loc, HD)
    keys_all = kv_image[:, :, 0]
    values_all = kv_image[:, :, 1]
    queries = query_low.reshape(img_loc, pat_loc, heads_loc, HD)
    factor = HD ** (-0.5)
    scores = (
        jnp.einsum("iqhd,ikhd->ihqk", queries, keys_all, preferred_element_type=jnp.float32)
        * factor
    )
    raised = jnp.exp(scores)
    attn_probs = raised / jnp.sum(raised, axis=-1, keepdims=True)
    probs_low = attn_probs.astype(jnp.bfloat16)
    attended = jnp.einsum(
        "ihqk,ikhd->iqhd", probs_low, values_all, preferred_element_type=jnp.float32
    ).astype(jnp.bfloat16)
    hidden_pre = branch_in[:, qkv_cols:]
    gelu_value, gelu_back = jax.vjp(gelu_exact, hidden_pre)
    activated = gelu_value.astype(jnp.bfloat16)
    branch_out = jnp.concatenate([attended.reshape(tok_loc, per_head), activated], axis=1)
    branch_rows = lax.all_gather(branch_out, "mx", axis=0, tiled=True)
    out_part = jnp.dot(
        branch_rows,
        lax.all_gather(second_local, "dp", axis=1, tiled=True),
        preferred_element_type=jnp.float32,
    )
    update_rows = lax.psum_scatter(
        out_part.astype(jnp.bfloat16), "my", scatter_dimension=1, tiled=True
    ).astype(jnp.float32)
    update = update_rows.reshape(image_total, pat_loc, width_loc).astype(jnp.bfloat16)
    grad_rows = lax.all_gather(cotangent.reshape(tok_dp, width_loc), "my", axis=1, tiled=True)
    col_block = grad_rows
    partial_out = contract_cols(col_block, lax.all_gather(second_local, "dp", axis=1, tiled=True))
    branch_grad = lax.psum_scatter(
        partial_out.astype(jnp.bfloat16), "mx", scatter_dimension=0, tiled=True
    ).astype(jnp.float32)
    out_grad = lax.psum_scatter(
        contract_rows(branch_rows, grad_rows).astype(jnp.bfloat16),
        "dp",
        scatter_dimension=1,
        tiled=True,
    )
    attn_grad = (
        branch_grad[:, :per_head].astype(jnp.bfloat16).reshape(img_loc, pat_loc, heads_loc, HD)
    )
    hid_grad = gelu_back(branch_grad[:, per_head:])[0].astype(jnp.bfloat16)
    value_part = jnp.einsum(
        "ihqk,iqhd->ikhd", probs_low, attn_grad, preferred_element_type=jnp.float32
    )
    prob_grad = jnp.einsum(
        "iqhd,ikhd->ihqk", attn_grad, values_all, preferred_element_type=jnp.float32
    )
    score_grad = attn_probs * (prob_grad - jnp.sum(attn_probs * prob_grad, axis=-1, keepdims=True))
    score_low = (score_grad * factor).astype(jnp.bfloat16)
    qn_grad = jnp.einsum(
        "ihqk,ikhd->iqhd", score_low, keys_all, preferred_element_type=jnp.float32
    ).reshape(tok_loc, heads_loc, HD)
    kn_part = jnp.einsum("ihqk,iqhd->ikhd", score_low, queries, preferred_element_type=jnp.float32)
    kv_part = jnp.stack([kn_part, value_part], axis=2).reshape(img_loc, PATCHES, 2 * per_head)
    kv_sums = (
        lax.psum_scatter(kv_part.astype(jnp.bfloat16), "dp", scatter_dimension=1, tiled=True)
        .astype(jnp.float32)
        .reshape(tok_loc, 2, heads_loc, HD)
    )
    value_grad = kv_sums[:, 1].astype(jnp.bfloat16)
    query_grad = head_norm_back(qn_grad, query_hat, query_inv).astype(jnp.bfloat16)
    key_grad = head_norm_back(kv_sums[:, 0], key_hat, key_inv).astype(jnp.bfloat16)
    stacked = jnp.stack([query_grad, key_grad, value_grad], axis=1).reshape(tok_loc, qkv_cols)
    input_grad = jnp.concatenate([stacked, hid_grad], axis=1)
    input_rows = lax.all_gather(input_grad, "mx", axis=0, tiled=True)
    col_block = features
    in_grad = lax.psum_scatter(
        contract_rows(col_block, input_rows).astype(jnp.bfloat16),
        "dp",
        scatter_dimension=0,
        tiled=True,
    )
    feat_part = contract_cols(input_rows, lax.all_gather(first_local, "dp", axis=0, tiled=True))
    feat_grad = lax.psum_scatter(
        feat_part.astype(jnp.bfloat16), "my", scatter_dimension=1, tiled=True
    ).astype(jnp.float32)
    sum_grad, sum_cross = lax.psum(
        (jnp.sum(feat_grad, axis=1), jnp.sum(feat_grad * standard, axis=1)), ("mx", "my")
    )
    tokens_grad = (
        inverse * (feat_grad - (sum_grad / D)[:, None] - standard * (sum_cross / D)[:, None])
    ).astype(jnp.bfloat16)
    tokens_grad = tokens_grad.reshape(image_total, pat_loc, width_loc)
    g_qkv = in_grad[:, :qkv_cols].reshape(local_rows, 3, per_head)
    g_up = in_grad[:, qkv_cols:]
    g_proj = out_grad[:per_head]
    g_down = out_grad[per_head:]
    return (update, tokens_grad, g_qkv, g_up, g_proj, g_down)


def solution(mesh):
    in_specs = (
        P(None, "dp", ("mx", "my")),
        P(("mx", "dp"), None, "my"),
        P(("mx", "dp"), "my"),
        P("my", ("mx", "dp")),
        P("my", ("mx", "dp")),
        P(None, "dp", ("mx", "my")),
    )
    out_specs = (
        P(None, "dp", ("mx", "my")),
        P(None, "dp", ("mx", "my")),
        P(("mx", "dp"), None, "my"),
        P(("mx", "dp"), "my"),
        P("my", ("mx", "dp")),
        P("my", ("mx", "dp")),
    )
    return jax.shard_map(body, mesh=mesh, in_specs=in_specs, out_specs=out_specs, check_vma=False)
```

profile of v0, /device:TPU:2, one launch (start us, length us, event | category | flops | bytes accessed | tf_op | source)
XLA Modules:
  0.0 818.5 jit_solution(9853465094821416267)
XLA Ops:
  7.2 1.1 copy.103
  8.4 2.1 pad_maximum_fusion
  10.6 0.9 pad_maximum_fusion.1
  11.8 154.6 %psum.28 = f32[512]{0:T(512)S(1)} all-reduce(f32[512]{0:T(512)S(1)} %reduce_sum.131), channel_id=1, replica_groups=mesh['dp'=4,'mx'=8,'my'=8] {'mx','my'}, use_global_device_ids=true, to_apply=%region_1.0 | all-reduce | flops 512 | bytes 4096 | tf_op jit(solution)/shard_map/psum | solution.py:56
  166.5 0.3 multiply_reduce_fusion.1
  166.9 152.3 %psum.29 = f32[512]{0:T(512)S(1)} all-reduce(f32[512]{0:T(512)S(1)} %reduce_sum.133), channel_id=1, replica_groups=mesh['dp'=4,'mx'=8,'my'=8] {'mx','my'}, use_global_device_ids=true, to_apply=%region_3.0 | all-reduce | flops 512 | bytes 4096 | tf_op jit(solution)/shard_map/psum | solution.py:58
  319.3 0.6 copy-done.10
  319.9 33.7 %all_gather.23 = bf16[512,768]{0,1:T(8,128)(2,1)S(1)} all-gather(bf16[512,96]{0,1:T(8,128)(2,1)S(1)} %fusion.33), channel_id=1, replica_groups=mesh['dp'=4,'mx'=8,'my'=8] {'my'}, dimensions={1}, use_global_device_ids=true | all-gather | bytes 884736 | tf_op jit(solution)/shard_map/all_gather | solution.py:63
  353.6 6.2 convolution_convert_fusion.1
  359.9 0.8 copy-done.5
  360.8 29.3 %all_gather.28 = bf16[512,768]{0,1:T(8,128)(2,1)S(1)} all-gather(bf16[512,96]{0,1:T(8,128)(2,1)S(1)} %copy.79), channel_id=1, replica_groups=mesh['dp'=4,'mx'=8,'my'=8] {'my'}, dimensions={1}, use_global_device_ids=true | all-gather | bytes 884736 | tf_op jit(solution)/shard_map/all_gather | solution.py:114
  390.1 5.0 fusion.1
  395.1 7.6 reduce-scatter.8.cloned.1.call-done
  402.8 0.9 slice.71
  404.5 0.3 copy-done.8
  405.5 7.8 all-gather
  413.6 0.3 fusion.45
  414.0 32.9 %reduce-scatter.12.cloned.1.call-done = bf16[64,1920]{1,0:T(8,128)(2,1)} async-done(((bf16[512,1920]{1,0:T(8,128)(2,1)}), bf16[64,1920]{1,0:T(8,128)(2,1)}) %reduce-scatter.12.cloned.1.call-update) | async-done | bytes 245776 | tf_op jit(solution)/shard_map/reduce_scatter | solution.py:117
  446.9 0.9 fusion.32
  447.9 0.4 fusion.6
  448.5 1.1 fusion.7
  449.6 0.9 copy.83
  450.7 1.9 fusion.16
  452.9 0.7 pad_maximum_fusion.4
  453.7 1.4 fusion.40
  455.2 26.2 %reduce-scatter.14.cloned.1.call-done = bf16[1,64,768]{2,1,0:T(8,128)(2,1)} async-done(((bf16[1,256,768]{2,1,0:T(8,128)(2,1)}), bf16[1,64,768]{2,1,0:T(8,128)(2,1)}) %reduce-scatter.14.cloned.1.call-update) | async-done | bytes 98320 | tf_op jit(solution)/shard_map/reduce_scatter | solution.py:144
  481.4 0.9 reshape.206
  482.7 0.3 fusion.36
  483.3 0.8 pad_maximum_fusion.3
  484.1 40.6 %all-gather.8.cloned.1.call-done = bf16[512,1920]{1,0:T(8,128)(2,1)} async-done(((bf16[64,1920]{1,0:T(8,128)(2,1)}), bf16[512,1920]{1,0:T(8,128)(2,1)}) %all-gather.8.cloned.1.call-update) | async-done | bytes 1966096 | tf_op jit(solution)/shard_map/all_gather | solution.py:104
  524.7 5.1 convolution_convert_fusion.4
  529.9 0.2 reduce-scatter.16.cloned.1.call-start
  530.1 38.8 %all-gather.12.cloned.1.call-done = bf16[512,2688]{1,0:T(8,128)(2,1)} async-done(((bf16[64,2688]{1,0:T(8,128)(2,1)}), bf16[512,2688]{1,0:T(8,128)(2,1)}) %all-gather.12.cloned.1.call-update) | async-done | bytes 2752528 | tf_op jit(solution)/shard_map/all_gather | solution.py:153
  568.9 6.4 convolution_convert_fusion.5
  575.4 5.0 convolution_convert_fusion.2
  580.4 6.2 convolution_convert_fusion
  586.6 23.3 %reduce-scatter.10.cloned.1.call-done = bf16[512,96]{0,1:T(8,128)(2,1)} async-done(((bf16[512,768]{0,1:T(8,128)(2,1)}), bf16[512,96]{0,1:T(8,128)(2,1)}) %reduce-scatter.10.cloned.1.call-update) | async-done | bytes 98320 | tf_op jit(solution)/shard_map/reduce_scatter | solution.py:110
  609.9 1.7 copy.78
  611.6 40.8 %reduce-scatter.16.cloned.1.call-done = bf16[512,96]{0,1:T(8,128)(2,1)} async-done(((bf16[512,768]{0,1:T(8,128)(2,1)}), bf16[512,96]{0,1:T(8,128)(2,1)}) %reduce-scatter.16.cloned.1.call-update) | async-done | bytes 98320 | tf_op jit(solution)/shard_map/reduce_scatter | solution.py:162
  652.3 1.0 convert_reduce_fusion
  653.3 149.7 %all-reduce = (f32[512]{0:T(512)S(1)}, f32[512]{0:T(512)S(1)}) all-reduce(f32[512]{0:T(512)S(1)} %get-tuple-element.33, f32[512]{0:T(512)S(1)} %get-tuple-element.32), channel_id=1, replica_groups=mesh['dp'=4,'mx'=8,'my'=8] {'mx','my'}, use_global_device_ids=true, to_apply=%region_22.0 | all-reduce | flops 1024 | bytes 8192 | tf_op jit(solution)/shard_map/psum | solution.py:165
  802.9 0.9 fusion.30
  803.9 0.8 copy.87
  804.7 1.6 slice.84
  806.2 1.9 slice.85
  808.2 1.0 slice.82
  809.2 0.8 copy.137
  810.0 1.9 slice.83
  (106 shorter events, 4.4 us)
Async XLA Ops:
  7.2 3.4 copy-start.2
  7.2 3.4 copy-start.4
  7.2 346.4 %all-gather.6.cloned.1.call-start = ((), (), s32[]{:S(2)}) async-start(), calls=%async_computation.7 | async-start | bytes 5160960 | tf_op jit(solution)/shard_map/all_gather | solution.py:69
  8.4 3.2 copy-start.1
  10.5 379.6 %all-gather.10.cloned.1.call-start = ((), (), s32[]{:S(2)}) async-start(), calls=%async_computation.10 | async-start | bytes 3686400 | tf_op jit(solution)/shard_map/all_gather | solution.py:107
  11.5 391.2 %reduce-scatter.8.cloned.1.call-start = ((), (), s32[]{:S(2)}) async-start(), calls=%async_computation.8 | async-start | bytes 3096576 | tf_op jit(solution)/shard_map/reduce_scatter | solution.py:72
  166.4 152.9 %copy-start.6 = (f32[512]{0:T(512)}, f32[512]{0:T(512)S(1)}, u32[]{:S(2)}) copy-start(f32[512]{0:T(512)S(1)} %broadcast_multiply_fusion.8) | copy-start | bytes 6148
  319.3 0.6 copy-start.10
  359.8 0.9 copy-start.5
  359.8 87.1 %reduce-scatter.12.cloned.1.call-start = ((), (), s32[]{:S(2)}) async-start(), calls=%async_computation.12 | async-start | bytes 2211840 | tf_op jit(solution)/shard_map/reduce_scatter | solution.py:117
  395.1 86.3 %reduce-scatter.14.cloned.1.call-start = ((), (), s32[]{:S(2)}) async-start(), calls=%async_computation.13 | async-start | bytes 491520 | tf_op jit(solution)/shard_map/reduce_scatter | solution.py:144
  404.3 0.6 copy-start.8
  404.9 0.6 copy-start.14
  405.5 45.2 %copy-start = (bf16[64,2688]{1,0:T(8,128)(2,1)S(1)}, bf16[64,2688]{1,0:T(8,128)(2,1)}, u32[]{:S(2)}) copy-start(bf16[64,2688]{1,0:T(8,128)(2,1)} %reduce-scatter.8.cloned.1.call-done) | copy-start | bytes 1032196
  413.4 34.9 %copy-start.12 = (f32[64,3]{0,1:T(4,128)}, f32[64,3]{0,1:T(4,128)S(1)}, u32[]{:S(2)}) copy-start(f32[64,3]{0,1:T(4,128)S(1)} %broadcast_multiply_fusion.4) | copy-start | bytes 2308
  413.6 34.7 %copy-start.16 = (f32[64,3]{0,1:T(4,128)}, f32[64,3]{0,1:T(4,128)S(1)}, u32[]{:S(2)}) copy-start(f32[64,3]{0,1:T(4,128)S(1)} %add_rsqrt_fusion) | copy-start | bytes 2308
  447.9 0.7 copy-start.3
  450.6 3.1 copy-start.13
  450.6 3.1 copy-start.17
  450.6 31.9 %copy-start.9 = (f32[64,3]{0,1:T(4,128)S(1)}, f32[64,3]{0,1:T(4,128)}, u32[]{:S(2)}) copy-start(f32[64,3]{0,1:T(4,128)} %copy-done.8) | copy-start | bytes 2308
  450.6 31.9 %copy-start.15 = (f32[64,3]{0,1:T(4,128)S(1)}, f32[64,3]{0,1:T(4,128)}, u32[]{:S(2)}) copy-start(f32[64,3]{0,1:T(4,128)} %copy-done.14) | copy-start | bytes 2308
  450.6 74.1 %all-gather.8.cloned.1.call-start = ((), (), s32[]{:S(2)}) async-start(), calls=%async_computation.9 | async-start | bytes 2211840 | tf_op jit(solution)/shard_map/all_gather | solution.py:104
  453.6 115.3 %all-gather.12.cloned.1.call-start = ((), (), s32[]{:S(2)}) async-start(), calls=%async_computation.14 | async-start | bytes 3096576 | tf_op jit(solution)/shard_map/all_gather | solution.py:153
  484.1 125.8 %reduce-scatter.10.cloned.1.call-start = ((), (), s32[]{:S(2)}) async-start(), calls=%async_computation.11 | async-start | bytes 884736 | tf_op jit(solution)/shard_map/reduce_scatter | solution.py:110
  529.9 122.4 %reduce-scatter.16.cloned.1.call-start = ((), (), s32[]{:S(2)}) async-start(), calls=%async_computation.15 | async-start | bytes 884736 | tf_op jit(solution)/shard_map/reduce_scatter | solution.py:162
  575.3 229.3 %reduce-scatter.20.cloned.1.call-start = ((), (), s32[]{:S(2)}) async-start(), calls=%async_computation.17 | async-start | bytes 3686400 | tf_op jit(solution)/shard_map/reduce_scatter | solution.py:120
  580.4 227.8 %reduce-scatter.18.cloned.1.call-start = ((), (), s32[]{:S(2)}) async-start(), calls=%async_computation.16 | async-start | bytes 5160960 | tf_op jit(solution)/shard_map/reduce_scatter | solution.py:155
  586.6 65.7 %copy-start.7 = (f32[512]{0:T(512)S(1)}, f32[512]{0:T(512)}, u32[]{:S(2)}) copy-start(f32[512]{0:T(512)} %copy-done.6) | copy-start | bytes 6148
  586.6 65.7 %copy-start.11 = (f32[512]{0:T(512)S(1)}, f32[512]{0:T(512)}, u32[]{:S(2)}) copy-start(f32[512]{0:T(512)} %copy-done.10) | copy-start | bytes 6148
Sparse Core Ops, SparseCore 0:
  10.6 43.2 all-gather.5
  55.7 33.5 all-gather.9
  360.0 42.7 reduce-scatter.7
  405.4 41.4 reduce-scatter.11
  450.7 30.5 reduce-scatter.13
  483.6 41.1 all-gather.7
  527.1 41.7 all-gather.11
  571.5 38.3 reduce-scatter.9
  612.6 39.6 reduce-scatter.15
  655.0 47.9 reduce-scatter.19
  706.0 55.7 reduce-scatter.17
where the time goes:
time: 827 us; the launch traced here: 818 us
  blocking collectives  527 us (64%)
  waiting for transfers between devices  210 us (25%)
  matrix products  38.1 us (5%)
  local copies, waits for them, and re-layouts  17.5 us (2%)
  between operations  14.3 us (2%)
  other arithmetic  10.2 us (1%)
    psum x1, blocking collectives, body(): totals = lax.psum(jnp.sum(x_float, axis=1), ('mx', 'my'))  155 us
    psum x1, blocking collectives, body(): spread = lax.psum(jnp.sum(centered * centered, axis=1), ('mx', 'my'))  152 us
    psum x1, blocking collectives, body(): lax.psum((jnp.sum(feat_grad, axis=1), jnp.sum(feat_grad * standard, axis=...  150 us
    reduce_scatter x1, waiting for transfers between devices, body(): lax.psum_scatter(feat_part.astype(jnp.bfloat16), 'my', scatter_dimension=...  40.8 us
    all_gather x1, waiting for transfers between devices, body(): branch_rows = lax.all_gather(branch_out, 'mx', axis=0, tiled=True)  40.6 us
    all_gather x1, waiting for transfers between devices, body(): input_rows = lax.all_gather(input_grad, 'mx', axis=0, tiled=True)  38.8 us
    all_gather x1, blocking collectives, body(): features = lax.all_gather(normed, 'my', axis=1, tiled=True)  33.7 us
    reduce_scatter x1, waiting for transfers between devices, body(): lax.psum_scatter(partial_out.astype(jnp.bfloat16), 'mx', scatter_dimensio...  32.9 us
  transfers between devices with their start and end apart: 11, of which 7 were waited for; matrix products, arithmetic and copies ran while one was open for 6% of the time, Pallas kernels for 0%

commit v1 on v0

v1 whole, which is shorter than its diff:
```python
import functools

import jax
import jax.numpy as jnp
from jax import lax
from jax.experimental import pallas as pl
from jax.experimental.pallas import tpu as pltpu
from jax.sharding import PartitionSpec as P

MESH = pl.DeviceIdType.MESH
F32, BF16 = jnp.float32, jnp.bfloat16

D = 6144
HD = 128
EPS = 1e-06
DP, MX, MY = 4, 8, 8
IMG, PAT = 8, 64
TOK = IMG * PAT
FW = 96
KB = MY * FW
KS = KB // DP
CW = 384
NC = 12
HEADS = CW // HD
FACTOR = HD ** (-0.5)
AG0 = 12
LAST = AG0 + NC + 4

NN = (((1,), (0,)), ((), ()))
NT = (((1,), (1,)), ((), ()))


def dot(a, b, dims=NN):
    return lax.dot_general(a, b, dims, preferred_element_type=F32)


def rcopy(src, dst, ssem, rsem, dev):
    return pltpu.make_async_remote_copy(
        src_ref=src, dst_ref=dst, send_sem=ssem, recv_sem=rsem, device_id=dev, device_id_type=MESH
    )


def rs_id(c):
    one = jnp.int32(1)
    ge4 = jnp.where(c >= 4, one, 0)
    ge8 = jnp.where(c >= 8, one, 0)
    return c + 4 * ge4 - 8 * ge8


def kind(i):
    return jnp.where((i < 4) | (i == 8), 0, 1).astype(jnp.int32)


def head_norm(x):
    hats, invs = [], []
    for h in range(HEADS):
        part = x[:, h * HD : (h + 1) * HD]
        cen = part - jnp.mean(part, axis=1, keepdims=True)
        inv = lax.rsqrt(jnp.mean(cen * cen, axis=1, keepdims=True) + EPS)
        hats.append(cen * inv)
        invs.append(jnp.broadcast_to(inv, cen.shape))
    return jnp.concatenate(hats, axis=1), jnp.concatenate(invs, axis=1)


def head_norm_back(up, hat, inv):
    outs = []
    for h in range(HEADS):
        s = slice(h * HD, (h + 1) * HD)
        u, n = up[:, s], hat[:, s]
        outs.append(
            inv[:, s]
            * (u - jnp.mean(u, axis=1, keepdims=True) - n * jnp.mean(u * n, axis=1, keepdims=True))
        )
    return jnp.concatenate(outs, axis=1)


def kernel(
    xt, ct, w, upd, tgr, gout,
    wg, part, rsl, rss, br, rows, fm, ft, std, acc, gp, gc, gs, gx,
    stage, yrec, xsend, xrec, st_own, st_in, st_fin, st_tot, fs_own, fs_z, fs_mid, fs_y,
    qlow, kvg, kvp, kvr, hats, qn,
    loc_sem, my_ss, my_rs, w_ss, w_rs, rl_ss, rl_rs, rsh_ss, rsh_rs, al_ss, al_rs, ash_ss, ash_rs,
    g_ss, g_rs, kv_ss, kv_rs, kp_ss, kp_rs, y_ss, y_rs, x_ss, x_rs, st_ss, st_rs, fz_ss, fz_rs, fy_ss, fy_rs,
):
    dp, m, my = lax.axis_index("dp"), lax.axis_index("mx"), lax.axis_index("my")
    xh, co = dp // 2, lax.rem(dp, 2)
    xl, yy = my // 4, lax.rem(my, 4)
    dp_x = lax.rem(dp + 2, 4)
    dp_c = xh * 2 + 1 - co
    my_x = lax.rem(my + 4, 8)

    def at_dp(i):
        return {"dp": i, "mx": m, "my": my}

    def at_mx(i):
        return {"dp": dp, "mx": lax.rem(i + 16, 8), "my": my}

    def at_my(i):
        return {"dp": dp, "mx": m, "my": i}

    def y_of(k):
        return lax.rem(yy + k, 4)

    barrier = pltpu.get_barrier_semaphore()
    peers = [at_dp(lax.rem(dp + k, 4)) for k in (1, 2, 3)]
    peers += [at_mx(m + k) for k in range(1, 8)]
    peers += [at_my(lax.rem(my + k, 8)) for k in range(1, 8)]
    for p in peers:
        pl.semaphore_signal(barrier, inc=1, device_id=p, device_id_type=MESH)

    own_w = pltpu.make_async_copy(w, wg.at[:, dp], loc_sem.at[0])
    own_c = pltpu.make_async_copy(ct, ft.at[0, my], loc_sem.at[1])
    own_x = pltpu.make_async_copy(xt, ft.at[1, my], loc_sem.at[2])
    own_c.start()
    own_w.start()
    own_x.start()
    acc[...] = jnp.zeros_like(acc)
    pl.semaphore_wait(barrier, len(peers))

    def my_first(j, src):
        return rcopy(src, ft.at[j, my], my_ss.at[j, 0], my_rs.at[j, 0], at_my(my_x))

    def my_own(j, k, src):
        return rcopy(src, ft.at[j, my], my_ss.at[j, k], my_rs.at[j, k], at_my(xl * 4 + y_of(k)))

    def my_fwd(j, k):
        return rcopy(ft.at[j, my_x], ft.at[j, my_x], my_ss.at[j, 3 + k], my_rs.at[j, 3 + k], at_my(xl * 4 + y_of(k)))

    def my_wait_first(j):
        rcopy(ft.at[j, my_x], ft.at[j, my_x], my_ss.at[j, 0], my_rs.at[j, 0], at_my(my_x)).wait_recv()

    def my_wait(j):
        for k in (1, 3, 2):
            a = xl * 4 + y_of(4 - k)
            b = (1 - xl) * 4 + y_of(4 - k)
            rcopy(ft.at[j, a], ft.at[j, a], my_ss.at[j, k], my_rs.at[j, k], at_my(my_x)).wait_recv()
            rcopy(ft.at[j, b], ft.at[j, b], my_ss.at[j, 3 + k], my_rs.at[j, 3 + k], at_my(my_x)).wait_recv()

    def w_x(i):
        return rcopy(w.at[i], wg.at[i, dp], w_ss.at[i, 0], w_rs.at[i, 0], at_dp(dp_x))

    def w_c(i):
        return rcopy(w.at[i], wg.at[i, dp], w_ss.at[i, 1], w_rs.at[i, 1], at_dp(dp_c))

    def w_f(i):
        return rcopy(wg.at[i, dp_x], wg.at[i, dp_x], w_ss.at[i, 2], w_rs.at[i, 2], at_dp(dp_c))

    def w_wait(i, step, who):
        rcopy(wg.at[i, who], wg.at[i, who], w_ss.at[i, step], w_rs.at[i, step], at_dp(dp_c)).wait_recv()

    my_first(0, ct).start()
    for k in (1, 3, 2):
        my_own(0, k, ct).start()

    def w_start(c, _):
        i = rs_id(c)
        w_x(i).start()
        w_c(i).start()
        return 0

    lax.fori_loop(0, NC, w_start, 0)
    my_first(1, xt).start()
    my_wait_first(0)
    for k in (1, 3, 2):
        my_fwd(0, k).start()
    for k in (1, 3, 2):
        my_own(1, k, xt).start()
    my_wait_first(1)
    for k in (1, 3, 2):
        my_fwd(1, k).start()
    own_w.wait()
    own_c.wait()
    own_x.wait()

    def w_forward(i):
        w_wait(i, 0, dp_x)
        w_f(i).start()

    w_forward(jnp.int32(0))
    my_wait(0)
    fm[0] = jnp.transpose(ft[0].reshape(KB, TOK), (1, 0))

    def stats_send():
        my_wait(1)
        for k in (1, 3, 2):
            my_fwd(1, k).wait_send()
        xs = ft[1].reshape(KB, TOK).astype(F32)
        std[...] = xs
        total = jnp.sum(xs, axis=0, keepdims=True)
        cen = xs - total * (1.0 / KB)
        st_own[0:1, :] = total
        st_own[1:2, :] = jnp.sum(cen * cen, axis=0, keepdims=True)
        for k in range(1, 8):
            rcopy(st_own, st_in.at[k - 1], st_ss.at[k - 1], st_rs.at[k - 1], at_mx(m + k)).start()

    def stats_done():
        for k in range(1, 8):
            rcopy(st_own, st_in.at[k - 1], st_ss.at[k - 1], st_rs.at[k - 1], at_mx(m + k)).wait()
        total = st_own[0:1, :]
        for k in range(7):
            total = total + st_in[k, 0:1, :]
        mean = total * (1.0 / D)
        spread = jnp.zeros_like(mean)
        for k in range(8):
            s, q = (st_own[0:1, :], st_own[1:2, :]) if k == 7 else (st_in[k, 0:1, :], st_in[k, 1:2, :])
            off = s * (1.0 / KB) - mean
            spread = spread + q + KB * off * off
        inv = lax.rsqrt(spread * (1.0 / D) + EPS)
        st_tot[0:1, :] = mean
        st_tot[1:2, :] = inv
        for j in range(MY):
            r = slice(j * FW, (j + 1) * FW)
            s = (std[r, :] - mean) * inv
            std[r, :] = s
            ft[1, j] = s.astype(BF16)
        fm[1] = jnp.transpose(ft[1].reshape(KB, TOK), (1, 0))

    def attn_open():
        q_hat, q_inv = head_norm(br[9])
        k_hat, k_inv = head_norm(br[10])
        hats[0], hats[1], hats[2], hats[3] = q_hat, q_inv, k_hat, k_inv
        qlow[...] = q_hat.astype(BF16)
        kvg[dp, :, :CW] = k_hat.astype(BF16)
        kvg[dp, :, CW:] = br[11].astype(BF16)
        for k in (1, 2, 3):
            rcopy(kvg.at[dp], kvg.at[dp], kv_ss.at[k - 1], kv_rs.at[k - 1], at_dp(lax.rem(dp + k, 4))).start()

    def attn_mid():
        for k in (1, 2, 3):
            s = lax.rem(dp + 4 - k, 4)
            rcopy(kvg.at[s], kvg.at[s], kv_ss.at[k - 1], kv_rs.at[k - 1], at_dp(dp_c)).wait_recv()
            rcopy(kvg.at[dp], kvg.at[dp], kv_ss.at[k - 1], kv_rs.at[k - 1], at_dp(dp_c)).wait_send()
        for h in range(HEADS):
            s = slice(h * HD, (h + 1) * HD)
            q = qlow[:, s]
            keys = kvg[:, :, s].reshape(DP * PAT, HD)
            vals = kvg[:, :, CW + h * HD : CW + (h + 1) * HD].reshape(DP * PAT, HD)
            ag = br[8, :, s].astype(BF16)
            raised = jnp.exp(dot(q, keys, NT) * FACTOR)
            probs = raised / jnp.sum(raised, axis=1, keepdims=True)
            plow = probs.astype(BF16)
            rows[8, m, :, s] = dot(plow, vals).astype(BF16)
            pgrad = dot(ag, vals, NT)
            sgrad = probs * (pgrad - jnp.sum(probs * pgrad, axis=1, keepdims=True))
            slow = (sgrad * FACTOR).astype(BF16)
            qn[:, s] = dot(slow, keys)
            vpart = dot(jnp.transpose(plow.astype(F32), (1, 0)).astype(BF16), ag)
            kpart = dot(jnp.transpose(slow.astype(F32), (1, 0)).astype(BF16), q)
            kvp[:, :, s] = kpart.astype(BF16).reshape(DP, PAT, HD)
            kvp[:, :, CW + h * HD : CW + (h + 1) * HD] = vpart.astype(BF16).reshape(DP, PAT, HD)
        for k in (1, 2, 3):
            t = lax.rem(dp + k, 4)
            rcopy(kvp.at[t], kvr.at[k - 1], kp_ss.at[k - 1], kp_rs.at[k - 1], at_dp(t)).start()

    def attn_close():
        sums = kvp[dp].astype(F32)
        for k in (1, 2, 3):
            t = lax.rem(dp + k, 4)
            rcopy(kvp.at[t], kvr.at[k - 1], kp_ss.at[k - 1], kp_rs.at[k - 1], at_dp(t)).wait()
            sums = sums + kvr[k - 1].astype(F32)
        rows[9, m] = head_norm_back(qn[...], hats[0], hats[1]).astype(BF16)
        rows[10, m] = head_norm_back(sums[:, :CW], hats[2], hats[3]).astype(BF16)
        rows[11, m] = sums[:, CW:].astype(BF16)

    def y_copy(j, k, half):
        t = half * 4 + y_of(k)
        return rcopy(
            stage.at[j, t], yrec.at[j, k - 1, half], y_ss.at[j, k - 1, half], y_rs.at[j, k - 1, half], at_my(xl * 4 + y_of(k))
        )

    def x_copy(j):
        return rcopy(xsend.at[j], xrec.at[j], x_ss.at[j], x_rs.at[j], at_my(my_x))

    def sum_open(j):
        stage[j] = acc[j].astype(BF16)
        for k in (1, 3, 2):
            for half in (0, 1):
                y_copy(j, k, half).start()

    def sum_mid(j):
        total = acc[j, my_x]
        for k in (1, 3, 2):
            for half in (0, 1):
                y_copy(j, k, half).wait()
        for k in (1, 2, 3):
            total = total + yrec[j, k - 1, 1 - xl].astype(F32)
        xsend[j] = total.astype(BF16)
        x_copy(j).start()

    def sum_close(j):
        total = acc[j, my]
        for k in (1, 2, 3):
            total = total + yrec[j, k - 1, xl].astype(F32)
        x_copy(j).wait()
        return total + xrec[j].astype(F32)

    def sign(c):
        return 1 - 2 * lax.rem(c, 2)

    def img(x):
        return lax.rem(x + 16, 8)

    def rl(c, step):
        i, g = rs_id(c), sign(c)
        b = part.at[i, img(m - g * (4 - step))]
        return rcopy(b, rsl.at[i, step], rl_ss.at[c, step], rl_rs.at[c, step], at_mx(m - g))

    def rsh(c, step):
        i, g = rs_id(c), sign(c)
        b = part.at[i, img(m + g * (3 - step))]
        return rcopy(b, rss.at[i, step], rsh_ss.at[c, step], rsh_rs.at[c, step], at_mx(m + g))

    def rs_middle(c, s):
        i, g = rs_id(c), sign(c)
        rl(c, s - 1).wait_recv()
        b = img(m - g * (4 - s))
        part[i, b] = (part[i, b].astype(F32) + rsl[i, s - 1].astype(F32)).astype(BF16)
        rl(c, s).start()
        if s <= 2:
            rsh(c, s - 1).wait_recv()
            b = img(m + g * (3 - s))
            part[i, b] = (part[i, b].astype(F32) + rss[i, s - 1].astype(F32)).astype(BF16)
            rsh(c, s).start()

    def rs_open(c):
        i = rs_id(c)
        w_wait(i, 1, dp_c)
        w_wait(i, 2, xh * 0 + 3 - dp)
        wv = wg[i].reshape(KB, CW)
        j = kind(i)
        for half in range(2):
            res = dot(fm[j, half * 256 : (half + 1) * 256, :], wv).astype(BF16)
            part[i, half * 4 : (half + 1) * 4] = res.reshape(4, PAT, CW)
        rl(c, 0).start()
        rsh(c, 0).start()

    def rs_final(c):
        i = rs_id(c)
        rl(c, 3).wait_recv()
        rsh(c, 2).wait_recv()
        br[i] = part[i, m].astype(F32) + rsl[i, 3].astype(F32) + rss[i, 2].astype(F32)

    def gelu(c):
        i = rs_id(c)
        u = br[i]
        phi = 0.5 + 0.5 * lax.erf(u * 0.7071067811865476)
        rows[i - 4, m] = (u * phi).astype(BF16)
        slope = phi + u * (0.3989422804014327 * jnp.exp(-0.5 * u * u))
        rows[i, m] = (br[i - 4] * slope).astype(BF16)

    def al(a, step):
        g = sign(a)
        b = rows.at[a, img(m + g * step)]
        return rcopy(b, b, al_ss.at[a, step], al_rs.at[a, step], at_mx(m - g))

    def ash(a, step):
        g = sign(a)
        b = rows.at[a, img(m - g * step)]
        return rcopy(b, b, ash_ss.at[a, step], ash_rs.at[a, step], at_mx(m + g))

    def al_wait(a, step):
        b = rows.at[a, img(m + sign(a) * (step + 1))]
        rcopy(b, b, al_ss.at[a, step], al_rs.at[a, step], at_mx(m + 1)).wait_recv()

    def ash_wait(a, step):
        b = rows.at[a, img(m - sign(a) * (step + 1))]
        rcopy(b, b, ash_ss.at[a, step], ash_rs.at[a, step], at_mx(m + 1)).wait_recv()

    def g_c(a, h):
        return rcopy(gp.at[a, h * 2 + 1 - co], gc.at[a, h], g_ss.at[a, h], g_rs.at[a, h], at_dp(dp_c))

    def g_x(a):
        return rcopy(gs.at[a], gx.at[a], g_ss.at[a, 2], g_rs.at[a, 2], at_dp(dp_x))

    def g_open(a):
        al_wait(a, 3)
        ash_wait(a, 2)
        r = rows[a].reshape(TOK, CW)
        j = kind(a)
        for h in range(4):
            gp[a, h] = dot(ft[j, 2 * h : 2 * h + 2].reshape(KS, TOK), r).astype(BF16)
        for h in range(2):
            g_c(a, h).start()
        for h in range(4):
            v = dot(wg[a, h], r, NT).reshape(2, FW, TOK)
            acc[j, 2 * h : 2 * h + 2] = acc[j, 2 * h : 2 * h + 2] + v

    def g_mid(a):
        for h in range(2):
            g_c(a, h).wait()
        gs[a] = (gp[a, dp_x].astype(F32) + gc[a, 1 - xh].astype(F32)).astype(BF16)
        g_x(a).start()

    def g_close(a):
        g_x(a).wait()
        gout[a] = (gp[a, dp].astype(F32) + gc[a, xh].astype(F32) + gx[a].astype(F32)).astype(BF16)

    def when_in(v, lo, hi):
        return pl.when((v >= lo) & (v < hi))

    def tick(t, _):
        for s in (3, 2, 1):
            when_in(t - s, 0, NC)(functools.partial(rs_middle, t - s, s))

        for s in (3, 2, 1):
            a = t - AG0 - s

            @when_in(a, 0, NC)
            def _(a=a, s=s):
                al_wait(a, s - 1)
                al(a, s).start()
                if s <= 2:
                    ash_wait(a, s - 1)
                    ash(a, s).start()

        @pl.when(t + 1 < NC)
        def _():
            w_forward(rs_id(t + 1))

        when_in(t, 0, NC)(functools.partial(rs_open, t))

        @when_in(t - 4, 0, NC)
        def _():
            rs_final(t - 4)

        when_in(t - 4, 8, NC)(functools.partial(gelu, t - 4))

        @when_in(t - AG0, 0, NC)
        def _():
            al(t - AG0, 0).start()
            ash(t - AG0, 0).start()

        pl.when(t == 2)(stats_send)
        pl.when(t == 4)(stats_done)
        pl.when(t == 11)(attn_open)
        pl.when(t == 13)(attn_mid)
        pl.when(t == 16)(attn_close)

        when_in(t - AG0 - 4, 0, NC)(functools.partial(g_open, t - AG0 - 4))
        when_in(t - AG0 - 5, 0, NC - 1)(functools.partial(g_mid, t - AG0 - 5))
        when_in(t - AG0 - 7, 0, NC - 3)(functools.partial(g_close, t - AG0 - 7))

        pl.when(t == AG0 + 13)(functools.partial(sum_open, 0))
        pl.when(t == AG0 + 15)(functools.partial(sum_mid, 0))

        for s in (4, 3, 2, 1):
            c = t - s

            @when_in(c, 0, NC)
            def _(c=c, s=s):
                rl(c, s - 1).wait_send()
                if s <= 3:
                    rsh(c, s - 1).wait_send()

            a = t - AG0 - s

            @when_in(a, 0, NC)
            def _(a=a, s=s):
                al(a, s - 1).wait_send()
                if s <= 3:
                    ash(a, s - 1).wait_send()

        return 0

    lax.fori_loop(0, LAST, tick, 0)

    sum_open(1)
    fsum = jnp.zeros((1, TOK), F32)
    fcross = jnp.zeros((1, TOK), F32)
    for j in range(MY):
        v = acc[1, j]
        fsum = fsum + jnp.sum(v, axis=0, keepdims=True)
        fcross = fcross + jnp.sum(v * std[j * FW : (j + 1) * FW, :], axis=0, keepdims=True)
    fs_own[0:1, :] = fsum
    fs_own[1:2, :] = fcross

    def fz(k):
        return rcopy(fs_own, fs_z.at[k - 1], fz_ss.at[k - 1], fz_rs.at[k - 1], at_mx(m + k))

    def fy(k):
        return rcopy(fs_mid, fs_y.at[k - 1], fy_ss.at[k - 1], fy_rs.at[k - 1], at_my(lax.rem(my + k, 8)))

    for k in range(1, 8):
        fz(k).start()
    g_mid(NC - 1)
    upd[...] = sum_close(0).astype(BF16)
    for k in range(1, 8):
        fz(k).wait()
    tot = fs_own[...]
    for k in range(7):
        tot = tot + fs_z[k]
    fs_mid[...] = tot
    for k in range(1, 8):
        fy(k).start()
    g_close(NC - 3)
    g_close(NC - 2)
    g_close(NC - 1)
    sum_mid(1)
    for k in range(1, 8):
        fy(k).wait()
    tot = fs_mid[...]
    for k in range(7):
        tot = tot + fs_y[k]
    mean_g = tot[0:1, :] * (1.0 / D)
    mean_c = tot[1:2, :] * (1.0 / D)
    fg = sum_close(1)
    own = std[pl.ds(pl.multiple_of(my * FW, FW), FW), :]
    tgr[...] = (st_tot[1:2, :] * (fg - mean_g - own * mean_c)).astype(BF16)

    for j, src in ((0, ct), (1, xt)):
        my_first(j, src).wait_send()
        for k in (1, 3, 2):
            my_own(j, k, src).wait_send()
    for k in (1, 3, 2):
        my_fwd(0, k).wait_send()

    def w_done(i, _):
        w_x(i).wait_send()
        w_c(i).wait_send()
        w_f(i).wait_send()
        return 0

    lax.fori_loop(0, NC, w_done, 0)


def fused(xt, ct, w):
    vm, sem = pltpu.VMEM, pltpu.SemaphoreType.DMA
    scratch = [
        vm((NC, DP, KS, CW), BF16),
        vm((NC, IMG, PAT, CW), BF16),
        vm((NC, 4, PAT, CW), BF16),
        vm((NC, 3, PAT, CW), BF16),
        vm((NC, PAT, CW), F32),
        vm((NC, IMG, PAT, CW), BF16),
        vm((2, TOK, KB), BF16),
        vm((2, MY, FW, TOK), BF16),
        vm((KB, TOK), F32),
        vm((2, MY, FW, TOK), F32),
        vm((NC, DP, KS, CW), BF16),
        vm((NC, 2, KS, CW), BF16),
        vm((NC, KS, CW), BF16),
        vm((NC, KS, CW), BF16),
        vm((2, MY, FW, TOK), BF16),
        vm((2, 3, 2, FW, TOK), BF16),
        vm((2, FW, TOK), BF16),
        vm((2, FW, TOK), BF16),
        vm((2, TOK), F32),
        vm((7, 2, TOK), F32),
        vm((7, 2, TOK), F32),
        vm((2, TOK), F32),
        vm((2, TOK), F32),
        vm((7, 2, TOK), F32),
        vm((2, TOK), F32),
        vm((7, 2, TOK), F32),
        vm((PAT, CW), BF16),
        vm((DP, PAT, 2 * CW), BF16),
        vm((DP, PAT, 2 * CW), BF16),
        vm((3, PAT, 2 * CW), BF16),
        vm((4, PAT, CW), F32),
        vm((PAT, CW), F32),
        sem((3,)),
        sem((2, 7)), sem((2, 7)),
        sem((NC, 3)), sem((NC, 3)),
        sem((NC, 4)), sem((NC, 4)),
        sem((NC, 3)), sem((NC, 3)),
        sem((NC, 4)), sem((NC, 4)),
        sem((NC, 3)), sem((NC, 3)),
        sem((NC, 3)), sem((NC, 3)),
        sem((3,)), sem((3,)),
        sem((3,)), sem((3,)),
        sem((2, 3, 2)), sem((2, 3, 2)),
        sem((2,)), sem((2,)),
        sem((7,)), sem((7,)),
        sem((7,)), sem((7,)),
        sem((7,)), sem((7,)),
    ]
    whole = pl.BlockSpec(memory_space=pltpu.VMEM)
    return pl.pallas_call(
        kernel,
        out_shape=(
            jax.ShapeDtypeStruct((FW, TOK), BF16),
            jax.ShapeDtypeStruct((FW, TOK), BF16),
            jax.ShapeDtypeStruct((NC, KS, CW), BF16),
        ),
        in_specs=[whole] * 3,
        out_specs=(whole,) * 3,
        scratch_shapes=scratch,
        compiler_params=pltpu.CompilerParams(
            collective_id=0, has_side_effects=True, vmem_limit_bytes=60 * 2**20
        ),
    )(xt, ct, w)


def body(tokens, w_qkv, w_up, w_proj, w_down, cotangent):
    xt = tokens.reshape(TOK, FW).T
    ct = cotangent.reshape(TOK, FW).T
    w = jnp.concatenate(
        [
            w_down.reshape(4, CW, KS).transpose(0, 2, 1),
            w_up.reshape(KS, 4, CW).transpose(1, 0, 2),
            w_proj.T[None],
            w_qkv.transpose(1, 0, 2),
        ],
        axis=0,
    )
    upd, tgr, g = fused(xt, ct, w)
    update = upd.T.reshape(IMG, PAT, FW)
    tokens_grad = tgr.T.reshape(IMG, PAT, FW)
    g_down = g[0:4].transpose(0, 2, 1).reshape(4 * CW, KS)
    g_up = g[4:8].transpose(1, 0, 2).reshape(KS, 4 * CW)
    g_proj = g[8].T
    g_qkv = g[9:12].transpose(1, 0, 2)
    return (update, tokens_grad, g_qkv, g_up, g_proj, g_down)


def solution(mesh):
    in_specs = (
        P(None, "dp", ("mx", "my")),
        P(("mx", "dp"), None, "my"),
        P(("mx", "dp"), "my"),
        P("my", ("mx", "dp")),
        P("my", ("mx", "dp")),
        P(None, "dp", ("mx", "my")),
    )
    out_specs = (
        P(None, "dp", ("mx", "my")),
        P(None, "dp", ("mx", "my")),
        P(("mx", "dp"), None, "my"),
        P(("mx", "dp"), "my"),
        P("my", ("mx", "dp")),
        P("my", ("mx", "dp")),
    )
    return jax.shard_map(body, mesh=mesh, in_specs=in_specs, out_specs=out_specs, check_vma=False)
```

time: 827 us -> 219 us (0.26)
  blocking collectives: 527 us -> 0 us
  waiting for transfers between devices: 210 us -> 0 us
  Pallas kernels: 0 us -> 199 us
  matrix products: 38.1 us -> 0 us
  between operations: 14.3 us -> 0.69 us
  other arithmetic: 10.2 us -> 1.55 us
    psum x3 -> x0, blocking collectives: 457 us -> none  [the longest x1 155 us: body(): totals = lax.psum(jnp.sum(x_float, axis=1), ('mx', 'my'))]
    pallas_call x0 -> x1, Pallas kernels: none -> 199 us  [fused(): pl.pallas_call(kernel, out_shape=(jax.ShapeDtypeStruct((FW, TOK), BF16),...]
    reduce_scatter x7 -> x0, waiting for transfers between devices: 131 us -> none  [the longest x1 40.8 us: body(): lax.psum_scatter(feat_part.astype(jnp.bfloat16), 'my', scatter_dimension=...]
    all_gather x4 -> x0, waiting for transfers between devices: 79.5 us -> none  [the longest x1 40.6 us: body(): branch_rows = lax.all_gather(branch_out, 'mx', axis=0, tiled=True)]
    all_gather x3 -> x0, blocking collectives: 70.8 us -> none  [the longest x1 33.7 us: body(): features = lax.all_gather(normed, 'my', axis=1, tiled=True)]
    dot_general x11 -> x0, matrix products: 37.8 us -> none  [the longest x2 11.3 us: contract_cols(): lax.dot_general(left_side, right_side, (((1,), (1,)), ((), ())), preferre...]
  transfers between devices with their start and end apart: 11 -> 0, of which waited for: 7 -> 0; matrix products, arithmetic and copies ran while one was open for 6% -> 0% of each run, Pallas kernels for 0% -> 0%
where the time goes in v1:
time: 219 us; the launch traced here: 215 us
  Pallas kernels  199 us (91%)
  local copies, waits for them, and re-layouts  14.5 us (7%)
    pallas_call x1, Pallas kernels, fused(): pl.pallas_call(kernel, out_shape=(jax.ShapeDtypeStruct((FW, TOK), BF16),...  199 us

profile of v1, /device:TPU:2, one launch (start us, length us, event | category | flops | bytes accessed | tf_op | source)
XLA Modules:
  0.0 215.3 jit_solution(3724186641918386299)
XLA Ops:
  0.6 0.0 copy-start.1
  0.6 0.0 copy-start
  0.7 1.7 copy.16
  2.4 1.6 copy.17
  4.0 1.4 bitcast_bitcast_fusion
  5.4 0.0 copy-done.1
  5.4 0.0 copy-done
  5.4 1.6 pad_maximum_fusion.w
  7.0 198.5 %shard_map.109 = (bf16[96,512]{1,0:T(8,128)(2,1)}, bf16[96,512]{1,0:T(8,128)(2,1)}, bf16[12,192,384]{2,1,0:T(8,128)(2,1)}) custom-call(bf16[96,512]{1,0:T(8,128)(2,1)} %bitcast.41, bf16[96,512]{1,0:T(8,128)(2,1)} %bitcast.42, bf16[12,192,384]{2,1,0:T(8,128)(2,1)} %pad_maximum_fusion.w), custom_call_target="tpu_custom_call" | custom-call | tf_op jit(solution)/shard_map/pallas_call | solution.py:578
  205.5 1.7 copy.21
  207.1 1.7 copy.20
  208.8 1.6 slice_bitcast_fusion.3
  210.4 1.8 slice_bitcast_fusion.2
  212.2 1.4 slice_bitcast_fusion
  213.6 0.9 copy.27
  214.4 0.9 copy.26
Async XLA Ops:
  0.6 4.7 %copy-start.1 = (bf16[384,192]{0,1:T(8,128)(2,1)S(1)}, bf16[384,192]{0,1:T(8,128)(2,1)}, u32[]{:S(2)}) copy-start(bf16[384,192]{0,1:T(8,128)(2,1)} %param.9) | copy-start | bytes 442372
  0.6 4.7 %copy-start = (bf16[192,3,384]{2,0,1:T(8,128)(2,1)S(1)}, bf16[192,3,384]{2,0,1:T(8,128)(2,1)}, u32[]{:S(2)}) copy-start(bf16[192,3,384]{2,0,1:T(8,128)(2,1)} %param.7) | copy-start | bytes 1327108

commit v2 on v1

--- a/solution.py
+++ b/solution.py
@@ -25,6 +25,7 @@
 FACTOR = HD ** (-0.5)
 AG0 = 12
 LAST = AG0 + NC + 4
+ORDER = (0, 1, 2, 3, 8, 9, 10, 11, 4, 5, 6, 7)
 
 NN = (((1,), (0,)), ((), ()))
 NT = (((1,), (1,)), ((), ()))
@@ -75,11 +76,12 @@
 
 
 def kernel(
-    xt, ct, w, upd, tgr, gout,
+    tok, cot, wd, wu, wp, wq, upd, tgr, gd, gu, gw, gq,
+    xraw, craw, xt, ct, gout,
     wg, part, rsl, rss, br, rows, fm, ft, std, acc, gp, gc, gs, gx,
     stage, yrec, xsend, xrec, st_own, st_in, st_fin, st_tot, fs_own, fs_z, fs_mid, fs_y,
     qlow, kvg, kvp, kvr, hats, qn,
-    loc_sem, my_ss, my_rs, w_ss, w_rs, rl_ss, rl_rs, rsh_ss, rsh_rs, al_ss, al_rs, ash_ss, ash_rs,
+    loc_sem, wl_sem, my_ss, my_rs, w_ss, w_rs, rl_ss, rl_rs, rsh_ss, rsh_rs, al_ss, al_rs, ash_ss, ash_rs,
     g_ss, g_rs, kv_ss, kv_rs, kp_ss, kp_rs, y_ss, y_rs, x_ss, x_rs, st_ss, st_rs, fz_ss, fz_rs, fy_ss, fy_rs,
 ):
     dp, m, my = lax.axis_index("dp"), lax.axis_index("mx"), lax.axis_index("my")
@@ -108,13 +110,26 @@
     for p in peers:
         pl.semaphore_signal(barrier, inc=1, device_id=p, device_id_type=MESH)
 
-    own_w = pltpu.make_async_copy(w, wg.at[:, dp], loc_sem.at[0])
-    own_c = pltpu.make_async_copy(ct, ft.at[0, my], loc_sem.at[1])
-    own_x = pltpu.make_async_copy(xt, ft.at[1, my], loc_sem.at[2])
+    def piece(i, down, up, proj, qkv):
+        if i < 4:
+            return down.at[:, i * CW : (i + 1) * CW]
+        if i < 8:
+            return up.at[:, (i - 4) * CW : (i - 3) * CW]
+        return proj if i == 8 else qkv.at[i - 9]
+
+    own_c = pltpu.make_async_copy(cot, craw, loc_sem.at[0])
+    own_x = pltpu.make_async_copy(tok, xraw, loc_sem.at[1])
     own_c.start()
-    own_w.start()
     own_x.start()
-    acc[...] = jnp.zeros_like(acc)
+    own_w = [pltpu.make_async_copy(piece(i, wd, wu, wp, wq), wg.at[i, dp], wl_sem.at[i]) for i in range(NC)]
+    for i in ORDER:
+        own_w[i].start()
+    own_c.wait()
+    ct[...] = jnp.transpose(craw[...].astype(F32), (1, 0)).astype(BF16)
+    ft[0, my] = ct[...]
+    own_x.wait()
+    xt[...] = jnp.transpose(xraw[...].astype(F32), (1, 0)).astype(BF16)
+    ft[1, my] = xt[...]
     pl.semaphore_wait(barrier, len(peers))
 
     def my_first(j, src):
@@ -137,10 +152,10 @@
             rcopy(ft.at[j, b], ft.at[j, b], my_ss.at[j, 3 + k], my_rs.at[j, 3 + k], at_my(my_x)).wait_recv()
 
     def w_x(i):
-        return rcopy(w.at[i], wg.at[i, dp], w_ss.at[i, 0], w_rs.at[i, 0], at_dp(dp_x))
+        return rcopy(wg.at[i, dp], wg.at[i, dp], w_ss.at[i, 0], w_rs.at[i, 0], at_dp(dp_x))
 
     def w_c(i):
-        return rcopy(w.at[i], wg.at[i, dp], w_ss.at[i, 1], w_rs.at[i, 1], at_dp(dp_c))
+        return rcopy(wg.at[i, dp], wg.at[i, dp], w_ss.at[i, 1], w_rs.at[i, 1], at_dp(dp_c))
 
     def w_f(i):
         return rcopy(wg.at[i, dp_x], wg.at[i, dp_x], w_ss.at[i, 2], w_rs.at[i, 2], at_dp(dp_c))
@@ -151,15 +166,12 @@
     my_first(0, ct).start()
     for k in (1, 3, 2):
         my_own(0, k, ct).start()
-
-    def w_start(c, _):
-        i = rs_id(c)
+    my_first(1, xt).start()
+    for i in ORDER:
+        own_w[i].wait()
         w_x(i).start()
         w_c(i).start()
-        return 0
-
-    lax.fori_loop(0, NC, w_start, 0)
-    my_first(1, xt).start()
+    acc[...] = jnp.zeros_like(acc)
     my_wait_first(0)
     for k in (1, 3, 2):
         my_fwd(0, k).start()
@@ -168,9 +180,6 @@
     my_wait_first(1)
     for k in (1, 3, 2):
         my_fwd(1, k).start()
-    own_w.wait()
-    own_c.wait()
-    own_x.wait()
 
     def w_forward(i):
         w_wait(i, 0, dp_x)
@@ -464,6 +473,9 @@
 
     lax.fori_loop(0, LAST, tick, 0)
 
+    out_copies = [pltpu.make_async_copy(gout.at[i], piece(i, gd, gu, gw, gq), wl_sem.at[i]) for i in range(NC)]
+    for i in range(NC - 3):
+        out_copies[i].start()
     sum_open(1)
     fsum = jnp.zeros((1, TOK), F32)
     fcross = jnp.zeros((1, TOK), F32)
@@ -483,7 +495,7 @@
     for k in range(1, 8):
         fz(k).start()
     g_mid(NC - 1)
-    upd[...] = sum_close(0).astype(BF16)
+    upd[...] = jnp.transpose(sum_close(0), (1, 0)).astype(BF16)
     for k in range(1, 8):
         fz(k).wait()
     tot = fs_own[...]
@@ -492,9 +504,9 @@
     fs_mid[...] = tot
     for k in range(1, 8):
         fy(k).start()
-    g_close(NC - 3)
-    g_close(NC - 2)
-    g_close(NC - 1)
+    for i in range(NC - 3, NC):
+        g_close(i)
+        out_copies[i].start()
     sum_mid(1)
     for k in range(1, 8):
         fy(k).wait()
@@ -505,7 +517,9 @@
     mean_c = tot[1:2, :] * (1.0 / D)
     fg = sum_close(1)
     own = std[pl.ds(pl.multiple_of(my * FW, FW), FW), :]
-    tgr[...] = (st_tot[1:2, :] * (fg - mean_g - own * mean_c)).astype(BF16)
+    tgr[...] = jnp.transpose(st_tot[1:2, :] * (fg - mean_g - own * mean_c), (1, 0)).astype(BF16)
+    for c in out_copies:
+        c.wait()
 
     for j, src in ((0, ct), (1, xt)):
         my_first(j, src).wait_send()
@@ -523,9 +537,14 @@
     lax.fori_loop(0, NC, w_done, 0)
 
 
-def fused(xt, ct, w):
+def fused(tok, cot, wd, wu, wp, wq):
     vm, sem = pltpu.VMEM, pltpu.SemaphoreType.DMA
     scratch = [
+        vm((TOK, FW), BF16),
+        vm((TOK, FW), BF16),
+        vm((FW, TOK), BF16),
+        vm((FW, TOK), BF16),
+        vm((NC, KS, CW), BF16),
         vm((NC, DP, KS, CW), BF16),
         vm((NC, IMG, PAT, CW), BF16),
         vm((NC, 4, PAT, CW), BF16),
@@ -558,7 +577,7 @@
         vm((3, PAT, 2 * CW), BF16),
         vm((4, PAT, CW), F32),
         vm((PAT, CW), F32),
-        sem((3,)),
+        sem((2,)), sem((NC,)),
         sem((2, 7)), sem((2, 7)),
         sem((NC, 3)), sem((NC, 3)),
         sem((NC, 4)), sem((NC, 4)),
@@ -575,42 +594,32 @@
         sem((7,)), sem((7,)),
     ]
     whole = pl.BlockSpec(memory_space=pltpu.VMEM)
+    far = pl.BlockSpec(memory_space=pl.ANY)
     return pl.pallas_call(
         kernel,
         out_shape=(
-            jax.ShapeDtypeStruct((FW, TOK), BF16),
-            jax.ShapeDtypeStruct((FW, TOK), BF16),
-            jax.ShapeDtypeStruct((NC, KS, CW), BF16),
+            jax.ShapeDtypeStruct((TOK, FW), BF16),
+            jax.ShapeDtypeStruct((TOK, FW), BF16),
+            jax.ShapeDtypeStruct((KS, 4 * CW), BF16),
+            jax.ShapeDtypeStruct((KS, 4 * CW), BF16),
+            jax.ShapeDtypeStruct((KS, CW), BF16),
+            jax.ShapeDtypeStruct((3, KS, CW), BF16),
         ),
-        in_specs=[whole] * 3,
-        out_specs=(whole,) * 3,
+        in_specs=[far] * 6,
+        out_specs=(whole, whole, far, far, far, far),
         scratch_shapes=scratch,
         compiler_params=pltpu.CompilerParams(
             collective_id=0, has_side_effects=True, vmem_limit_bytes=60 * 2**20
         ),
-    )(xt, ct, w)
+    )(tok, cot, wd, wu, wp, wq)
 
 
 def body(tokens, w_qkv, w_up, w_proj, w_down, cotangent):
-    xt = tokens.reshape(TOK, FW).T
-    ct = cotangent.reshape(TOK, FW).T
-    w = jnp.concatenate(
-        [
-            w_down.reshape(4, CW, KS).transpose(0, 2, 1),
-            w_up.reshape(KS, 4, CW).transpose(1, 0, 2),
-            w_proj.T[None],
-            w_qkv.transpose(1, 0, 2),
-        ],
-        axis=0,
+    upd, tgr, gd, gu, gw, gq = fused(
+        tokens.reshape(TOK, FW), cotangent.reshape(TOK, FW), w_down.T, w_up, w_proj.T, w_qkv.transpose(1, 0, 2)
     )
-    upd, tgr, g = fused(xt, ct, w)
-    update = upd.T.reshape(IMG, PAT, FW)
-    tokens_grad = tgr.T.reshape(IMG, PAT, FW)
-    g_down = g[0:4].transpose(0, 2, 1).reshape(4 * CW, KS)
-    g_up = g[4:8].transpose(1, 0, 2).reshape(KS, 4 * CW)
-    g_proj = g[8].T
-    g_qkv = g[9:12].transpose(1, 0, 2)
-    return (update, tokens_grad, g_qkv, g_up, g_proj, g_down)
+    shape = (IMG, PAT, FW)
+    return (upd.reshape(shape), tgr.reshape(shape), gq.transpose(1, 0, 2), gu, gw.T, gd.T)
 
 
 def solution(mesh):

time: 219 us -> 175 us (0.80); the launches traced: 215 us -> 175 us
  Pallas kernels: 199 us -> 168 us
  local copies, waits for them, and re-layouts: 14.5 us -> 6.52 us
    pallas_call x1, Pallas kernels: 199 us -> 168 us  [fused(): pl.pallas_call(kernel, out_shape=(jax.ShapeDtypeStruct((TOK, FW), BF16),...]
    transpose x5 -> x0, local copies, waits for them, and re-layouts: 8.08 us -> none  [the longest x1 1.82 us: body(): g_qkv = g[9:12].transpose(1, 0, 2)]
    unnamed x5 -> x14, local copies, waits for them, and re-layouts: 1.37 us -> 6.52 us
    reshape x4 -> x0, local copies, waits for them, and re-layouts: 5.09 us -> none  [the longest x1 1.7 us: body(): xt = tokens.reshape(TOK, FW).T]
where the time goes in v2:
time: 175 us
  Pallas kernels  168 us (96%)
  local copies, waits for them, and re-layouts  6.52 us (4%)
    pallas_call x1, Pallas kernels, fused(): pl.pallas_call(kernel, out_shape=(jax.ShapeDtypeStruct((TOK, FW), BF16),...  168 us
    unnamed x14, local copies, waits for them, and re-layouts  6.52 us

profile of v2, /device:TPU:2, one launch (start us, length us, event | category | flops | bytes accessed | tf_op | source)
XLA Modules:
  0.0 175.2 jit_solution(3236990401547366994)
XLA Ops:
  0.6 168.0 %shard_map.109 = (bf16[512,96]{1,0:T(8,128)(2,1)}, bf16[512,96]{1,0:T(8,128)(2,1)}, bf16[192,1536]{1,0:T(8,128)(2,1)}, bf16[192,1536]{1,0:T(8,128)(2,1)}, bf16[1...) custom-call(bf16[512,96]{1,0:T(8,128)(2,1)} %bitcast.16, bf16[512,96]{1,0:T(8,128)(2,1)} %bitcast.17, ...), custom_call_target="tpu_custom_call" | custom-call | tf_op jit(solution)/shard_map/pallas_call | solution.py:598
  168.6 0.0 copy-start.2
  168.6 1.6 copy.18
  170.3 0.0 copy-start.1
  170.3 1.6 copy.19
  171.9 0.0 copy-done.2
  171.9 0.8 copy.20
  172.7 0.0 copy-done.1
  172.7 0.0 copy-start.3
  172.7 0.0 copy-start
  172.7 0.8 copy.21
  173.5 0.2 copy-done.3
  173.7 0.7 copy.22
  174.3 0.0 copy-done
  174.4 0.8 copy.23
Async XLA Ops:
  168.6 3.3 %copy-start.2 = (bf16[3,192,384]{2,1,0:T(8,128)(2,1)S(1)}, bf16[3,192,384]{2,1,0:T(8,128)(2,1)}, u32[]{:S(2)}) copy-start(bf16[3,192,384]{2,1,0:T(8,128)(2,1)} %get-tuple-element.14) | copy-start | bytes 1327108
  170.3 2.4 %copy-start.1 = (bf16[192,1536]{1,0:T(8,128)(2,1)S(1)}, bf16[192,1536]{1,0:T(8,128)(2,1)}, u32[]{:S(2)}) copy-start(bf16[192,1536]{1,0:T(8,128)(2,1)} %get-tuple-element.27) | copy-start | bytes 1769476
  172.7 1.0 copy-start.3
  172.7 1.7 copy-start

commit v3 on v2

v3 whole, which is shorter than its diff:
```python
import functools

import jax
import jax.numpy as jnp
from jax import lax
from jax.experimental import pallas as pl
from jax.experimental.pallas import tpu as pltpu
from jax.sharding import PartitionSpec as P

MESH = pl.DeviceIdType.MESH
F32, BF16 = jnp.float32, jnp.bfloat16

D = 6144
HD = 128
EPS = 1e-06
DP, MX, MY = 4, 8, 8
IMG, PAT = 8, 64
TOK = IMG * PAT
HALF = PAT // 2
NP = IMG // 2
PT = 2 * PAT
FW = 96
KB = MY * FW
KS = KB // DP
CW = 384
NC = 12
HEADS = CW // HD
FACTOR = HD ** (-0.5)
AG0 = 12
LAST = AG0 + NC + 4
ORDER = (0, 1, 2, 3, 8, 9, 10, 11, 4, 5, 6, 7)

NN = (((1,), (0,)), ((), ()))
NT = (((1,), (1,)), ((), ()))


def dot(a, b, dims=NN):
    return lax.dot_general(a, b, dims, preferred_element_type=F32)


def rcopy(src, dst, ssem, rsem, dev):
    return pltpu.make_async_remote_copy(
        src_ref=src, dst_ref=dst, send_sem=ssem, recv_sem=rsem, device_id=dev, device_id_type=MESH
    )


def rs_id(c):
    one = jnp.int32(1)
    ge4 = jnp.where(c >= 4, one, 0)
    ge8 = jnp.where(c >= 8, one, 0)
    return c + 4 * ge4 - 8 * ge8


def kind(i):
    return jnp.where((i < 4) | (i == 8), 0, 1).astype(jnp.int32)


def head_norm(x):
    hats, invs = [], []
    for h in range(HEADS):
        part = x[:, h * HD : (h + 1) * HD]
        cen = part - jnp.mean(part, axis=1, keepdims=True)
        inv = lax.rsqrt(jnp.mean(cen * cen, axis=1, keepdims=True) + EPS)
        hats.append(cen * inv)
        invs.append(jnp.broadcast_to(inv, cen.shape))
    return jnp.concatenate(hats, axis=1), jnp.concatenate(invs, axis=1)


def head_norm_back(up, hat, inv):
    outs = []
    for h in range(HEADS):
        s = slice(h * HD, (h + 1) * HD)
        u, n = up[:, s], hat[:, s]
        outs.append(
            inv[:, s]
            * (u - jnp.mean(u, axis=1, keepdims=True) - n * jnp.mean(u * n, axis=1, keepdims=True))
        )
    return jnp.concatenate(outs, axis=1)


def kernel(
    tok, cot, wd, wu, wp, wq, upd, tgr, gd, gu, gw, gq,
    xraw, craw, gout,
    wg, part, rsd, rsu, br, rows, fm, ft, fl, std, acc, gp, gc, gs, gx,
    stage, yrec, xsend, xrec, st_own, st_in, st_tot, fs_own, fs_z, fs_mid, fs_y,
    qlow, kvg, kvp, kvr, hats, qn,
    loc_sem, wl_sem, my_ss, my_rs, w_ss, w_rs, rd_ss, rd_rs, ru_ss, ru_rs, ad_ss, ad_rs, au_ss, au_rs,
    g_ss, g_rs, kv_ss, kv_rs, kp_ss, kp_rs, y_ss, y_rs, x_ss, x_rs, st_ss, st_rs, fz_ss, fz_rs, fy_ss, fy_rs,
):
    dp, m, my = lax.axis_index("dp"), lax.axis_index("mx"), lax.axis_index("my")
    xh, co = dp // 2, lax.rem(dp, 2)
    xl, yy = my // 4, lax.rem(my, 4)
    dp_x = lax.rem(dp + 2, 4)
    dp_c = xh * 2 + 1 - co
    my_x = lax.rem(my + 4, 8)
    own_p = m // 2
    far_p, plus_p, minus_p = lax.rem(own_p + 2, 4), lax.rem(own_p + 1, 4), lax.rem(own_p + 3, 4)

    def at_dp(i):
        return {"dp": i, "mx": m, "my": my}

    def at_mx(i):
        return {"dp": dp, "mx": lax.rem(i + 16, 8), "my": my}

    def at_my(i):
        return {"dp": dp, "mx": m, "my": i}

    def y_of(k):
        return lax.rem(yy + k, 4)

    barrier = pltpu.get_barrier_semaphore()
    peers = [at_dp(lax.rem(dp + k, 4)) for k in (1, 2, 3)]
    peers += [at_mx(m + k) for k in range(1, 8)]
    peers += [at_my(lax.rem(my + k, 8)) for k in range(1, 8)]
    for p in peers:
        pl.semaphore_signal(barrier, inc=1, device_id=p, device_id_type=MESH)

    def piece(i, down, up, proj, qkv):
        if i < 4:
            return down.at[:, i * CW : (i + 1) * CW]
        if i < 8:
            return up.at[:, (i - 4) * CW : (i - 3) * CW]
        return proj if i == 8 else qkv.at[i - 9]

    own_c = pltpu.make_async_copy(cot, craw, loc_sem.at[0])
    own_x = pltpu.make_async_copy(tok, xraw, loc_sem.at[1])
    own_c.start()
    own_x.start()
    own_w = [pltpu.make_async_copy(piece(i, wd, wu, wp, wq), wg.at[i, dp], wl_sem.at[i]) for i in range(NC)]
    for i in ORDER:
        own_w[i].start()
    own_c.wait()
    for p in range(NP):
        ft[0, p, my] = jnp.transpose(craw[p * PT : (p + 1) * PT, :].astype(F32), (1, 0)).astype(BF16)
    own_x.wait()
    for p in range(NP):
        ft[1, p, my] = jnp.transpose(xraw[p * PT : (p + 1) * PT, :].astype(F32), (1, 0)).astype(BF16)
    pl.semaphore_wait(barrier, len(peers))

    def block(j, p, who):
        return ft.at[1, :, who] if j else ft.at[0, p, who]

    def slot(j, p):
        return NP if j else p

    def my_first(j, p):
        b, q = block(j, p, my), slot(j, p)
        return rcopy(b, b, my_ss.at[q, 0], my_rs.at[q, 0], at_my(my_x))

    def my_own(j, p, k):
        b, q = block(j, p, my), slot(j, p)
        return rcopy(b, b, my_ss.at[q, k], my_rs.at[q, k], at_my(xl * 4 + y_of(k)))

    def my_fwd(j, p, k):
        b, q = block(j, p, my_x), slot(j, p)
        return rcopy(b, b, my_ss.at[q, 3 + k], my_rs.at[q, 3 + k], at_my(xl * 4 + y_of(k)))

    def my_wait_first(j, p):
        b, q = block(j, p, my_x), slot(j, p)
        rcopy(b, b, my_ss.at[q, 0], my_rs.at[q, 0], at_my(my_x)).wait_recv()

    def my_wait(j, p):
        q = slot(j, p)
        for k in (1, 3, 2):
            a = block(j, p, xl * 4 + y_of(4 - k))
            b = block(j, p, (1 - xl) * 4 + y_of(4 - k))
            rcopy(a, a, my_ss.at[q, k], my_rs.at[q, k], at_my(my_x)).wait_recv()
            rcopy(b, b, my_ss.at[q, 3 + k], my_rs.at[q, 3 + k], at_my(my_x)).wait_recv()

    def my_sent(j, p):
        my_first(j, p).wait_send()
        for k in (1, 3, 2):
            my_own(j, p, k).wait_send()
            my_fwd(j, p, k).wait_send()

    def w_x(i):
        return rcopy(wg.at[i, dp], wg.at[i, dp], w_ss.at[i, 0], w_rs.at[i, 0], at_dp(dp_x))

    def w_c(i):
        return rcopy(wg.at[i, dp], wg.at[i, dp], w_ss.at[i, 1], w_rs.at[i, 1], at_dp(dp_c))

    def w_f(i):
        return rcopy(wg.at[i, dp_x], wg.at[i, dp_x], w_ss.at[i, 2], w_rs.at[i, 2], at_dp(dp_c))

    def w_wait(i, step, who):
        rcopy(wg.at[i, who], wg.at[i, who], w_ss.at[i, step], w_rs.at[i, step], at_dp(dp_c)).wait_recv()

    def w_forward(i):
        w_wait(i, 0, dp_x)
        w_f(i).start()

    def start_own(j, p):
        for k in (1, 3, 2):
            my_own(j, p, k).start()

    def start_fwd(j, p):
        my_wait_first(j, p)
        for k in (1, 3, 2):
            my_fwd(j, p, k).start()

    my_first(0, far_p).start()
    own_w[0].wait()
    w_x(0).start()
    w_c(0).start()
    start_own(0, far_p)
    for p in (plus_p, minus_p, own_p):
        my_first(0, p).start()
    own_w[1].wait()
    w_x(1).start()
    w_c(1).start()
    start_own(0, plus_p)
    start_fwd(0, far_p)
    start_own(0, minus_p)
    start_fwd(0, plus_p)
    my_first(1, 0).start()
    for i in ORDER[2:]:
        own_w[i].wait()
        w_x(i).start()
        w_c(i).start()
    start_own(0, own_p)
    start_fwd(0, minus_p)
    start_fwd(0, own_p)
    start_own(1, 0)
    acc[...] = jnp.zeros_like(acc)
    w_forward(jnp.int32(0))

    def cot_pair(p):
        my_wait(0, p)
        v = ft[0, p].reshape(KB, PT)
        fm[0, p] = jnp.transpose(v.astype(F32), (1, 0)).astype(BF16)

    def stats_send():
        my_wait(1, 0)
        my_sent(1, 0)
        for p in range(NP):
            xs = ft[1, p].reshape(KB, PT).astype(F32)
            std[p] = xs
            total = jnp.sum(xs, axis=0, keepdims=True)
            cen = xs - total * (1.0 / KB)
            st_own[0:1, p * PT : (p + 1) * PT] = total
            st_own[1:2, p * PT : (p + 1) * PT] = jnp.sum(cen * cen, axis=0, keepdims=True)
            fl[0, :, p * PT : (p + 1) * PT] = ft[0, p].reshape(KB, PT)
        for k in range(1, 8):
            rcopy(st_own, st_in.at[k - 1], st_ss.at[k - 1], st_rs.at[k - 1], at_mx(m + k)).start()

    def stats_done():
        for k in range(1, 8):
            rcopy(st_own, st_in.at[k - 1], st_ss.at[k - 1], st_rs.at[k - 1], at_mx(m + k)).wait()
        total = st_own[0:1, :]
        for k in range(7):
            total = total + st_in[k, 0:1, :]
        mean = total * (1.0 / D)
        spread = jnp.zeros_like(mean)
        for k in range(8):
            s, q = (st_own[0:1, :], st_own[1:2, :]) if k == 7 else (st_in[k, 0:1, :], st_in[k, 1:2, :])
            off = s * (1.0 / KB) - mean
            spread = spread + q + KB * off * off
        inv = lax.rsqrt(spread * (1.0 / D) + EPS)
        st_tot[...] = inv
        for p in range(NP):
            c = slice(p * PT, (p + 1) * PT)
            v = (std[p] - mean[:, c]) * inv[:, c]
            std[p] = v
            fl[1, :, c] = v.astype(BF16)
            fm[1, p] = jnp.transpose(v, (1, 0)).astype(BF16)

    def attn_open():
        q_hat, q_inv = head_norm(br[9])
        k_hat, k_inv = head_norm(br[10])
        hats[0], hats[1], hats[2], hats[3] = q_hat, q_inv, k_hat, k_inv
        qlow[...] = q_hat.astype(BF16)
        kvg[dp, :, :CW] = k_hat.astype(BF16)
        kvg[dp, :, CW:] = br[11].astype(BF16)
        for k in (1, 2, 3):
            rcopy(kvg.at[dp], kvg.at[dp], kv_ss.at[k - 1], kv_rs.at[k - 1], at_dp(lax.rem(dp + k, 4))).start()

    def attn_mid():
        for k in (1, 2, 3):
            s = lax.rem(dp + 4 - k, 4)
            rcopy(kvg.at[s], kvg.at[s], kv_ss.at[k - 1], kv_rs.at[k - 1], at_dp(dp_c)).wait_recv()
            rcopy(kvg.at[dp], kvg.at[dp], kv_ss.at[k - 1], kv_rs.at[k - 1], at_dp(dp_c)).wait_send()
        for h in range(HEADS):
            s = slice(h * HD, (h + 1) * HD)
            q = qlow[:, s]
            keys = kvg[:, :, s].reshape(DP * PAT, HD)
            vals = kvg[:, :, CW + h * HD : CW + (h + 1) * HD].reshape(DP * PAT, HD)
            ag = br[8, :, s].astype(BF16)
            raised = jnp.exp(dot(q, keys, NT) * FACTOR)
            probs = raised / jnp.sum(raised, axis=1, keepdims=True)
            plow = probs.astype(BF16)
            rows[8, m, :, s] = dot(plow, vals).astype(BF16)
            pgrad = dot(ag, vals, NT)
            sgrad = probs * (pgrad - jnp.sum(probs * pgrad, axis=1, keepdims=True))
            slow = (sgrad * FACTOR).astype(BF16)
            qn[:, s] = dot(slow, keys)
            vpart = dot(jnp.transpose(plow.astype(F32), (1, 0)).astype(BF16), ag)
            kpart = dot(jnp.transpose(slow.astype(F32), (1, 0)).astype(BF16), q)
            kvp[:, :, s] = kpart.astype(BF16).reshape(DP, PAT, HD)
            kvp[:, :, CW + h * HD : CW + (h + 1) * HD] = vpart.astype(BF16).reshape(DP, PAT, HD)
        for k in (1, 2, 3):
            t = lax.rem(dp + k, 4)
            rcopy(kvp.at[t], kvr.at[k - 1], kp_ss.at[k - 1], kp_rs.at[k - 1], at_dp(t)).start()

    def attn_close():
        sums = kvp[dp].astype(F32)
        for k in (1, 2, 3):
            t = lax.rem(dp + k, 4)
            rcopy(kvp.at[t], kvr.at[k - 1], kp_ss.at[k - 1], kp_rs.at[k - 1], at_dp(t)).wait()
            sums = sums + kvr[k - 1].astype(F32)
        rows[9, m] = head_norm_back(qn[...], hats[0], hats[1]).astype(BF16)
        rows[10, m] = head_norm_back(sums[:, :CW], hats[2], hats[3]).astype(BF16)
        rows[11, m] = sums[:, CW:].astype(BF16)

    def y_copy(j, p, k):
        return rcopy(
            stage.at[j, p, y_of(k)], yrec.at[j, p, k - 1], y_ss.at[j, p, k - 1], y_rs.at[j, p, k - 1], at_my(xl * 4 + y_of(k))
        )

    def x_copy(j, p):
        return rcopy(xsend.at[j, p], xrec.at[j, p], x_ss.at[j, p], x_rs.at[j, p], at_my(my_x))

    def sum_open(j, p):
        for y in range(4):
            for half in range(2):
                stage[j, p, y, half] = acc[j, p, half * 4 + y].astype(BF16)
        for k in (1, 3, 2):
            y_copy(j, p, k).start()
        if j:
            v = acc[1, p].reshape(KB, PT)
            fs_own[p, 0:1, :] = jnp.sum(v, axis=0, keepdims=True)
            fs_own[p, 1:2, :] = jnp.sum(v * std[p], axis=0, keepdims=True)

    def sum_mid(j, p):
        total = acc[j, p, my_x]
        for k in (1, 3, 2):
            y_copy(j, p, k).wait()
        for k in (1, 2, 3):
            total = total + yrec[j, p, k - 1, 1 - xl].astype(F32)
        xsend[j, p] = total.astype(BF16)
        x_copy(j, p).start()

    def sum_close(j, p):
        total = acc[j, p, my]
        for k in (1, 2, 3):
            total = total + yrec[j, p, k - 1, xl].astype(F32)
        x_copy(j, p).wait()
        return total + xrec[j, p].astype(F32)

    def img(x):
        return lax.rem(x + 16, 8)

    def halfd(ref, s):
        return ref.at[pl.ds(0, HALF)] if s == 0 else ref

    def halfu(ref, s):
        return ref.at[pl.ds(HALF, HALF)] if s == 0 else ref

    def rd(c, s):
        i = rs_id(c)
        return rcopy(
            halfd(part.at[i, img(m - 4 + s)], s), halfd(rsd.at[i, s], s), rd_ss.at[c, s], rd_rs.at[c, s], at_mx(m - 1)
        )

    def ru(c, s):
        i = rs_id(c)
        return rcopy(
            halfu(part.at[i, img(m + 4 - s)], s), halfu(rsu.at[i, s], s), ru_ss.at[c, s], ru_rs.at[c, s], at_mx(m + 1)
        )

    def rs_middle(c, s):
        i = rs_id(c)
        lo, hi = (slice(0, HALF), slice(HALF, PAT)) if s == 1 else (slice(0, PAT), slice(0, PAT))
        rd(c, s - 1).wait_recv()
        b = img(m - 4 + s)
        part[i, b, lo] = (part[i, b, lo].astype(F32) + rsd[i, s - 1, lo].astype(F32)).astype(BF16)
        rd(c, s).start()
        ru(c, s - 1).wait_recv()
        b = img(m + 4 - s)
        part[i, b, hi] = (part[i, b, hi].astype(F32) + rsu[i, s - 1, hi].astype(F32)).astype(BF16)
        ru(c, s).start()

    def rs_pair(c, p):
        i = rs_id(c)
        res = dot(fm[kind(i), p], wg[i].reshape(KB, CW)).astype(BF16)
        part[i, pl.ds(2 * p, 2)] = res.reshape(2, PAT, CW)

    def rs_open(c):
        i = rs_id(c)
        w_wait(i, 1, dp_c)
        w_wait(i, 2, 3 - dp)
        rs_pair(c, far_p)
        rd(c, 0).start()
        ru(c, 0).start()

    def rs_final(c):
        i = rs_id(c)
        rd(c, 3).wait_recv()
        ru(c, 3).wait_recv()
        br[i] = part[i, m].astype(F32) + rsd[i, 3].astype(F32) + rsu[i, 3].astype(F32)

    def gelu(c):
        i = rs_id(c)
        u = br[i]
        phi = 0.5 + 0.5 * lax.erf(u * 0.7071067811865476)
        rows[i - 4, m] = (u * phi).astype(BF16)
        slope = phi + u * (0.3989422804014327 * jnp.exp(-0.5 * u * u))
        rows[i, m] = (br[i - 4] * slope).astype(BF16)

    def ad(a, s):
        b = halfd(rows.at[a, img(m + s)], 3 - s)
        return rcopy(b, b, ad_ss.at[a, s], ad_rs.at[a, s], at_mx(m - 1))

    def au(a, s):
        b = halfu(rows.at[a, img(m - s)], 3 - s)
        return rcopy(b, b, au_ss.at[a, s], au_rs.at[a, s], at_mx(m + 1))

    def ad_wait(a, s):
        b = halfd(rows.at[a, img(m + s + 1)], 3 - s)
        rcopy(b, b, ad_ss.at[a, s], ad_rs.at[a, s], at_mx(m - 1)).wait_recv()

    def au_wait(a, s):
        b = halfu(rows.at[a, img(m - s - 1)], 3 - s)
        rcopy(b, b, au_ss.at[a, s], au_rs.at[a, s], at_mx(m + 1)).wait_recv()

    def ag_open(a):
        ad(a, 0).start()
        au(a, 0).start()

    def ag_middle(a, s):
        ad_wait(a, s - 1)
        ad(a, s).start()
        au_wait(a, s - 1)
        au(a, s).start()

    def ag_pair(a, p):
        r = rows[a, pl.ds(2 * p, 2)].reshape(PT, CW)
        j = kind(a)
        acc[j, p] = acc[j, p] + dot(wg[a].reshape(KB, CW), r, NT).reshape(MY, FW, PT)

    def g_c(a, h):
        return rcopy(gp.at[a, h * 2 + 1 - co], gc.at[a, h], g_ss.at[a, h], g_rs.at[a, h], at_dp(dp_c))

    def g_x(a):
        return rcopy(gs.at[a], gx.at[a], g_ss.at[a, 2], g_rs.at[a, 2], at_dp(dp_x))

    def ag_far(a):
        ad_wait(a, 3)
        au_wait(a, 3)
        ag_pair(a, far_p)

    def g_open(a):
        r = rows[a].reshape(TOK, CW)
        j = kind(a)
        for h in range(4):
            gp[a, h] = dot(fl[j, h * KS : (h + 1) * KS, :], r).astype(BF16)
        for h in range(2):
            g_c(a, h).start()

    def g_mid(a):
        for h in range(2):
            g_c(a, h).wait()
        gs[a] = (gp[a, dp_x].astype(F32) + gc[a, 1 - xh].astype(F32)).astype(BF16)
        g_x(a).start()

    def g_close(a):
        g_x(a).wait()
        gout[a] = (gp[a, dp].astype(F32) + gc[a, xh].astype(F32) + gx[a].astype(F32)).astype(BF16)

    def when_in(v, lo, hi):
        return pl.when((v >= lo) & (v < hi))

    def tick(t, _):
        u = t - AG0
        for s in (3, 2, 1):
            when_in(t - s, 0, NC)(functools.partial(rs_middle, t - s, s))
        for s in (3, 2, 1):
            when_in(u - s, 0, NC)(functools.partial(ag_middle, u - s, s))

        @pl.when(u == NC + 3)
        def _():
            ag_far(u - 4)
            sum_open(1, far_p)

        @pl.when(t + 1 < NC)
        def _():
            w_forward(rs_id(t + 1))

        @pl.when(t == 0)
        def _():
            cot_pair(far_p)

        when_in(t, 0, NC)(functools.partial(rs_open, t))

        @when_in(t - 4, 0, NC)
        def _():
            rs_final(t - 4)

        when_in(t - 4, 8, NC)(functools.partial(gelu, t - 4))
        when_in(u, 0, NC)(functools.partial(ag_open, u))

        @pl.when(t == 0)
        def _():
            cot_pair(plus_p)
            cot_pair(minus_p)

        @when_in(t, 0, NC)
        def _():
            rs_pair(t, plus_p)
            rs_pair(t, minus_p)

        @pl.when(t == 1)
        def _():
            cot_pair(own_p)
            start_fwd(1, 0)

        @when_in(t - 1, 0, NC)
        def _():
            rs_pair(t - 1, own_p)

        pl.when(t == 3)(stats_send)
        pl.when(t == 4)(stats_done)
        pl.when(t == 11)(attn_open)
        pl.when(t == 13)(attn_mid)
        pl.when(t == 16)(attn_close)

        when_in(u - 4, 0, NC - 1)(functools.partial(ag_far, u - 4))

        @when_in(u - 3, 0, NC)
        def _():
            ag_pair(u - 3, plus_p)
            ag_pair(u - 3, minus_p)

        when_in(u - 1, 0, NC)(functools.partial(ag_pair, u - 1, own_p))

        when_in(u - 4, 0, NC)(functools.partial(g_open, u - 4))
        when_in(u - 5, 0, NC - 1)(functools.partial(g_mid, u - 5))
        when_in(u - 7, 0, NC - 3)(functools.partial(g_close, u - 7))

        for j, a in ((0, 8), (1, NC - 1)):
            pl.when(u == a + 1)(functools.partial(sum_open, j, own_p))

            @pl.when(u == a + 3)
            def _(j=j):
                sum_open(j, plus_p)
                sum_open(j, minus_p)
                sum_mid(j, own_p)

        pl.when(u == 12)(functools.partial(sum_open, 0, far_p))

        @pl.when(u == 13)
        def _():
            sum_mid(0, plus_p)
            sum_mid(0, minus_p)

        pl.when(u == 14)(functools.partial(sum_mid, 0, far_p))

        for s in (4, 3, 2, 1):
            c = t - s

            @when_in(c, 0, NC)
            def _(c=c, s=s):
                rd(c, s - 1).wait_send()
                ru(c, s - 1).wait_send()

            a = u - s

            @when_in(a, 0, NC)
            def _(a=a, s=s):
                ad(a, s - 1).wait_send()
                au(a, s - 1).wait_send()

        return 0

    lax.fori_loop(0, LAST, tick, 0)

    def fz(k):
        return rcopy(fs_own, fs_z.at[k - 1], fz_ss.at[k - 1], fz_rs.at[k - 1], at_mx(m + k))

    def fy(k):
        return rcopy(fs_mid, fs_y.at[k - 1], fy_ss.at[k - 1], fy_rs.at[k - 1], at_my(lax.rem(my + k, 8)))

    for k in range(1, 8):
        fz(k).start()
    sum_mid(1, plus_p)
    sum_mid(1, minus_p)
    g_mid(NC - 1)
    out_copies = [pltpu.make_async_copy(gout.at[i], piece(i, gd, gu, gw, gq), wl_sem.at[i]) for i in range(NC)]
    for i in range(NC - 3):
        out_copies[i].start()
    for k in range(1, 8):
        fz(k).wait()
    tot = fs_own[...]
    for k in range(7):
        tot = tot + fs_z[k]
    fs_mid[...] = tot
    for k in range(1, 8):
        fy(k).start()
    sum_mid(1, far_p)
    for p in range(NP):
        upd[p * PT : (p + 1) * PT, :] = jnp.transpose(sum_close(0, p), (1, 0)).astype(BF16)
    for i in range(NC - 3, NC):
        g_close(i)
        out_copies[i].start()
    for k in range(1, 8):
        fy(k).wait()
    tot = fs_mid[...]
    for k in range(7):
        tot = tot + fs_y[k]
    tot = tot * (1.0 / D)
    for p in range(NP):
        own = std[p, pl.ds(pl.multiple_of(my * FW, FW), FW), :]
        grad = sum_close(1, p) - tot[p, 0:1, :] - own * tot[p, 1:2, :]
        tgr[p * PT : (p + 1) * PT, :] = jnp.transpose(st_tot[:, p * PT : (p + 1) * PT] * grad, (1, 0)).astype(BF16)
    for c in out_copies:
        c.wait()

    for p in range(NP):
        my_sent(0, p)

    def w_done(i, _):
        w_x(i).wait_send()
        w_c(i).wait_send()
        w_f(i).wait_send()
        return 0

    lax.fori_loop(0, NC, w_done, 0)


def copy_kernel(*refs):
    n = len(refs) // 2
    for i in range(n):
        refs[n + i][...] = refs[i][...]


def copied(*arrays):
    whole = pl.BlockSpec(memory_space=pltpu.VMEM)
    return pl.pallas_call(
        copy_kernel,
        out_shape=tuple(jax.ShapeDtypeStruct(a.shape, a.dtype) for a in arrays),
        in_specs=[whole] * len(arrays),
        out_specs=(whole,) * len(arrays),
        compiler_params=pltpu.CompilerParams(vmem_limit_bytes=16 * 2**20),
    )(*arrays)


def fused(tok, cot, wd, wu, wp, wq):
    vm, sem = pltpu.VMEM, pltpu.SemaphoreType.DMA
    scratch = [
        vm((TOK, FW), BF16),
        vm((TOK, FW), BF16),
        vm((NC, KS, CW), BF16),
        vm((NC, DP, KS, CW), BF16),
        vm((NC, IMG, PAT, CW), BF16),
        vm((NC, 4, PAT, CW), BF16),
        vm((NC, 4, PAT, CW), BF16),
        vm((NC, PAT, CW), F32),
        vm((NC, IMG, PAT, CW), BF16),
        vm((2, NP, PT, KB), BF16),
        vm((2, NP, MY, FW, PT), BF16),
        vm((2, KB, TOK), BF16),
        vm((NP, KB, PT), F32),
        vm((2, NP, MY, FW, PT), F32),
        vm((NC, DP, KS, CW), BF16),
        vm((NC, 2, KS, CW), BF16),
        vm((NC, KS, CW), BF16),
        vm((NC, KS, CW), BF16),
        vm((2, NP, 4, 2, FW, PT), BF16),
        vm((2, NP, 3, 2, FW, PT), BF16),
        vm((2, NP, FW, PT), BF16),
        vm((2, NP, FW, PT), BF16),
        vm((2, TOK), F32),
        vm((7, 2, TOK), F32),
        vm((1, TOK), F32),
        vm((NP, 2, PT), F32),
        vm((7, NP, 2, PT), F32),
        vm((NP, 2, PT), F32),
        vm((7, NP, 2, PT), F32),
        vm((PAT, CW), BF16),
        vm((DP, PAT, 2 * CW), BF16),
        vm((DP, PAT, 2 * CW), BF16),
        vm((3, PAT, 2 * CW), BF16),
        vm((4, PAT, CW), F32),
        vm((PAT, CW), F32),
        sem((2,)), sem((NC,)),
        sem((NP + 1, 7)), sem((NP + 1, 7)),
        sem((NC, 3)), sem((NC, 3)),
        sem((NC, 4)), sem((NC, 4)),
        sem((NC, 4)), sem((NC, 4)),
        sem((NC, 4)), sem((NC, 4)),
        sem((NC, 4)), sem((NC, 4)),
        sem((NC, 3)), sem((NC, 3)),
        sem((3,)), sem((3,)),
        sem((3,)), sem((3,)),
        sem((2, NP, 3)), sem((2, NP, 3)),
        sem((2, NP)), sem((2, NP)),
        sem((7,)), sem((7,)),
        sem((7,)), sem((7,)),
        sem((7,)), sem((7,)),
    ]
    whole = pl.BlockSpec(memory_space=pltpu.VMEM)
    far = pl.BlockSpec(memory_space=pl.ANY)
    return pl.pallas_call(
        kernel,
        out_shape=(
            jax.ShapeDtypeStruct((TOK, FW), BF16),
            jax.ShapeDtypeStruct((TOK, FW), BF16),
            jax.ShapeDtypeStruct((KS, 4 * CW), BF16),
            jax.ShapeDtypeStruct((KS, 4 * CW), BF16),
            jax.ShapeDtypeStruct((KS, CW), BF16),
            jax.ShapeDtypeStruct((3, KS, CW), BF16),
        ),
        in_specs=[far] * 6,
        out_specs=(whole, whole, far, far, far, far),
        scratch_shapes=scratch,
        compiler_params=pltpu.CompilerParams(
            collective_id=0, has_side_effects=True, vmem_limit_bytes=60 * 2**20
        ),
    )(tok, cot, wd, wu, wp, wq)


def body(tokens, w_qkv, w_up, w_proj, w_down, cotangent):
    upd, tgr, gd, gu, gw, gq = copied(
        *fused(tokens.reshape(TOK, FW), cotangent.reshape(TOK, FW), w_down.T, w_up, w_proj.T, w_qkv.transpose(1, 0, 2))
    )
    shape = (IMG, PAT, FW)
    return (upd.reshape(shape), tgr.reshape(shape), gq.transpose(1, 0, 2), gu, gw.T, gd.T)


def solution(mesh):
    in_specs = (
        P(None, "dp", ("mx", "my")),
        P(("mx", "dp"), None, "my"),
        P(("mx", "dp"), "my"),
        P("my", ("mx", "dp")),
        P("my", ("mx", "dp")),
        P(None, "dp", ("mx", "my")),
    )
    out_specs = (
        P(None, "dp", ("mx", "my")),
        P(None, "dp", ("mx", "my")),
        P(("mx", "dp"), None, "my"),
        P(("mx", "dp"), "my"),
        P("my", ("mx", "dp")),
        P("my", ("mx", "dp")),
    )
    return jax.shard_map(body, mesh=mesh, in_specs=in_specs, out_specs=out_specs, check_vma=False)
```

time: 175 us -> 172 us (0.983)
  Pallas kernels: 168 us -> 165 us
    pallas_call x1, Pallas kernels: 168 us -> 163 us  [fused(): pl.pallas_call(kernel, out_shape=(jax.ShapeDtypeStruct((TOK, FW), BF16),...]
    unnamed x14 -> x12, local copies, waits for them, and re-layouts: 6.52 us -> 5.85 us
where the time goes in v3:
time: 172 us; the launch traced here: 171 us
  Pallas kernels  165 us (96%)
  local copies, waits for them, and re-layouts  5.85 us (3%)
    pallas_call x1, Pallas kernels, fused(): pl.pallas_call(kernel, out_shape=(jax.ShapeDtypeStruct((TOK, FW), BF16),...  163 us
    unnamed x12, local copies, waits for them, and re-layouts  5.85 us

profile of v3, /device:TPU:2, one launch (start us, length us, event | category | flops | bytes accessed | tf_op | source)
XLA Modules:
  0.0 171.1 jit_solution(11101361095715836657)
XLA Ops:
  0.6 163.2 %shard_map.109 = (bf16[512,96]{1,0:T(8,128)(2,1)}, bf16[512,96]{1,0:T(8,128)(2,1)}, bf16[192,1536]{1,0:T(8,128)(2,1)}, bf16[192,1536]{1,0:T(8,128)(2,1)}, bf16[1...) custom-call(bf16[512,96]{1,0:T(8,128)(2,1)} %bitcast.13, bf16[512,96]{1,0:T(8,128)(2,1)} %bitcast.14, ...), custom_call_target="tpu_custom_call" | custom-call | tf_op jit(solution)/shard_map/pallas_call | solution.py:702
  163.8 0.0 copy-start
  163.8 1.1 copy-done
  164.9 0.0 copy-start.1
  164.9 1.1 copy-done.1
  165.9 0.0 copy-start.2
  165.9 1.0 copy-done.2
  166.9 0.0 copy-start.3
  166.9 0.9 copy-done.3
  167.9 0.0 copy-start.4
  167.9 0.9 copy-done.4
  168.8 0.0 copy-start.5
  168.8 0.9 copy-done.5
  169.7 1.5 shard_map.110
Async XLA Ops:
  163.8 1.1 copy-start
  164.9 1.1 copy-start.1
  165.9 1.0 copy-start.2
  166.9 0.9 copy-start.3
  167.9 0.9 copy-start.4
  168.8 0.9 copy-start.5

commit v4 on v3

--- a/solution.py
+++ b/solution.py
@@ -26,7 +26,8 @@
 NC = 12
 HEADS = CW // HD
 FACTOR = HD ** (-0.5)
-AG0 = 12
+POS = NC - 1
+AG0 = 11
 LAST = AG0 + NC + 4
 ORDER = (0, 1, 2, 3, 8, 9, 10, 11, 4, 5, 6, 7)
 
@@ -222,7 +223,6 @@
     start_fwd(0, own_p)
     start_own(1, 0)
     acc[...] = jnp.zeros_like(acc)
-    w_forward(jnp.int32(0))
 
     def cot_pair(p):
         my_wait(0, p)
@@ -384,11 +384,13 @@
         res = dot(fm[kind(i), p], wg[i].reshape(KB, CW)).astype(BF16)
         part[i, pl.ds(2 * p, 2)] = res.reshape(2, PAT, CW)
 
-    def rs_open(c):
+    def rs_far(c):
         i = rs_id(c)
         w_wait(i, 1, dp_c)
         w_wait(i, 2, 3 - dp)
         rs_pair(c, far_p)
+
+    def rs_send(c):
         rd(c, 0).start()
         ru(c, 0).start()
 
@@ -469,11 +471,32 @@
     def when_in(v, lo, hi):
         return pl.when((v >= lo) & (v < hi))
 
+    def at_pos(v, step, first=0):
+        @when_in(v, 0, POS)
+        def _():
+            def one(c, _):
+                step(c)
+                return 0
+
+            lax.fori_loop(jnp.where(v == 0, first, v + 1), v + 2, one, 0)
+
+    w_forward(jnp.int32(0))
+    cot_pair(far_p)
+    rs_far(jnp.int32(0))
+    rs_send(jnp.int32(0))
+    start_fwd(1, 0)
+    w_forward(jnp.int32(1))
+    rs_far(jnp.int32(1))
+
     def tick(t, _):
         u = t - AG0
-        for s in (3, 2, 1):
-            when_in(t - s, 0, NC)(functools.partial(rs_middle, t - s, s))
-        for s in (3, 2, 1):
+        at_pos(t, rs_send, first=1)
+        for s in (1, 2, 3):
+            at_pos(t - s, functools.partial(lambda s, c: rs_middle(c, s), s))
+        at_pos(t - 4, rs_final)
+        when_in(t - 3, 8, NC)(functools.partial(gelu, t - 3))
+        when_in(u, 0, NC)(functools.partial(ag_open, u))
+        for s in (1, 2, 3):
             when_in(u - s, 0, NC)(functools.partial(ag_middle, u - s, s))
 
         @pl.when(u == NC + 3)
@@ -481,47 +504,36 @@
             ag_far(u - 4)
             sum_open(1, far_p)
 
-        @pl.when(t + 1 < NC)
-        def _():
-            w_forward(rs_id(t + 1))
-
-        @pl.when(t == 0)
-        def _():
-            cot_pair(far_p)
-
-        when_in(t, 0, NC)(functools.partial(rs_open, t))
-
-        @when_in(t - 4, 0, NC)
-        def _():
-            rs_final(t - 4)
-
-        when_in(t - 4, 8, NC)(functools.partial(gelu, t - 4))
-        when_in(u, 0, NC)(functools.partial(ag_open, u))
-
         @pl.when(t == 0)
         def _():
             cot_pair(plus_p)
             cot_pair(minus_p)
 
-        @when_in(t, 0, NC)
+        @pl.when(t + 2 < NC)
         def _():
-            rs_pair(t, plus_p)
-            rs_pair(t, minus_p)
+            w_forward(rs_id(t + 2))
+
+        def sides(c):
+            rs_pair(c, plus_p)
+            rs_pair(c, minus_p)
+
+        at_pos(t, sides)
 
         @pl.when(t == 1)
         def _():
             cot_pair(own_p)
-            start_fwd(1, 0)
-
-        @when_in(t - 1, 0, NC)
+
+        at_pos(t - 1, lambda c: rs_pair(c, own_p))
+        pl.when(t == 3)(stats_done)
+
+        @pl.when(t + 2 < NC)
         def _():
-            rs_pair(t - 1, own_p)
-
-        pl.when(t == 3)(stats_send)
-        pl.when(t == 4)(stats_done)
-        pl.when(t == 11)(attn_open)
-        pl.when(t == 13)(attn_mid)
-        pl.when(t == 16)(attn_close)
+            rs_far(t + 2)
+
+        pl.when(t == 2)(stats_send)
+        pl.when(t == 10)(attn_open)
+        pl.when(t == 12)(attn_mid)
+        pl.when(t == 15)(attn_close)
 
         when_in(u - 4, 0, NC - 1)(functools.partial(ag_far, u - 4))
 
@@ -555,13 +567,12 @@
         pl.when(u == 14)(functools.partial(sum_mid, 0, far_p))
 
         for s in (4, 3, 2, 1):
-            c = t - s
-
-            @when_in(c, 0, NC)
-            def _(c=c, s=s):
+
+            def sent(c, s=s):
                 rd(c, s - 1).wait_send()
                 ru(c, s - 1).wait_send()
 
+            at_pos(t - s, sent)
             a = u - s
 
             @when_in(a, 0, NC)
@@ -627,19 +638,30 @@
 
 
 def copy_kernel(*refs):
-    n = len(refs) // 2
+    n = (len(refs) - 2) // 3
+    src, dst, held = refs[:n], refs[n : 2 * n], refs[2 * n : 3 * n]
+    sin, sout = refs[3 * n :]
+    come = [pltpu.make_async_copy(src[i], held[i], sin.at[i]) for i in range(n)]
+    go = [pltpu.make_async_copy(held[i], dst[i], sout.at[i]) for i in range(n)]
+    for c in come:
+        c.start()
     for i in range(n):
-        refs[n + i][...] = refs[i][...]
+        come[i].wait()
+        go[i].start()
+    for c in go:
+        c.wait()
 
 
 def copied(*arrays):
-    whole = pl.BlockSpec(memory_space=pltpu.VMEM)
+    far = pl.BlockSpec(memory_space=pl.ANY)
+    n = len(arrays)
     return pl.pallas_call(
         copy_kernel,
         out_shape=tuple(jax.ShapeDtypeStruct(a.shape, a.dtype) for a in arrays),
-        in_specs=[whole] * len(arrays),
-        out_specs=(whole,) * len(arrays),
-        compiler_params=pltpu.CompilerParams(vmem_limit_bytes=16 * 2**20),
+        in_specs=[far] * n,
+        out_specs=(far,) * n,
+        scratch_shapes=[pltpu.VMEM(a.shape, a.dtype) for a in arrays] + [pltpu.SemaphoreType.DMA((n,))] * 2,
+        compiler_params=pltpu.CompilerParams(vmem_limit_bytes=60 * 2**20),
     )(*arrays)
 
 

time: 172 us -> 156 us (0.907)
  Pallas kernels: 165 us -> 155 us
  local copies, waits for them, and re-layouts: 5.85 us -> 0 us
    pallas_call x1, Pallas kernels: 163 us -> 152 us  [fused(): pl.pallas_call(kernel, out_shape=(jax.ShapeDtypeStruct((TOK, FW), BF16),...]
    unnamed x12 -> x0, local copies, waits for them, and re-layouts: 5.85 us -> none
where the time goes in v4:
time: 156 us; the launch traced here: 155 us
  Pallas kernels  155 us (99%)
    pallas_call x1, Pallas kernels, fused(): pl.pallas_call(kernel, out_shape=(jax.ShapeDtypeStruct((TOK, FW), BF16),...  152 us

profile of v4, /device:TPU:2, one launch (start us, length us, event | category | flops | bytes accessed | tf_op | source)
XLA Modules:
  0.0 155.5 jit_solution(17479742291339705776)
XLA Ops:
  0.6 152.3 %shard_map.109 = (bf16[512,96]{1,0:T(8,128)(2,1)}, bf16[512,96]{1,0:T(8,128)(2,1)}, bf16[192,1536]{1,0:T(8,128)(2,1)}, bf16[192,1536]{1,0:T(8,128)(2,1)}, bf16[1...) custom-call(bf16[512,96]{1,0:T(8,128)(2,1)} %bitcast.13, bf16[512,96]{1,0:T(8,128)(2,1)} %bitcast.14, ...), custom_call_target="tpu_custom_call" | custom-call | tf_op jit(solution)/shard_map/pallas_call | solution.py:724
  153.0 2.5 %shard_map.110 = (bf16[512,96]{1,0:T(8,128)(2,1)}, bf16[512,96]{1,0:T(8,128)(2,1)}, bf16[192,1536]{1,0:T(8,128)(2,1)}, bf16[192,1536]{1,0:T(8,128)(2,1)}, bf16[1...) custom-call(bf16[512,96]{1,0:T(8,128)(2,1)} %get-tuple-element.18.refs_0_, bf16[512,96]{1,0:T(8,128)(2,1)} %get-tuple-element.19.refs_1_, ...), custom_call_target="tpu_custom_call" | custom-call | tf_op jit(solution)/shard_map/pallas_call | solution.py:658

commit v5 on v4

--- a/solution.py
+++ b/solution.py
@@ -27,8 +27,8 @@
 HEADS = CW // HD
 FACTOR = HD ** (-0.5)
 POS = NC - 1
-AG0 = 11
-LAST = AG0 + NC + 4
+AG0 = 12
+LAST = AG0 + NC + 3
 ORDER = (0, 1, 2, 3, 8, 9, 10, 11, 4, 5, 6, 7)
 
 NN = (((1,), (0,)), ((), ()))
@@ -490,28 +490,26 @@
 
     def tick(t, _):
         u = t - AG0
+
+        def middle(s):
+            at_pos(t - s, lambda c: rs_middle(c, s))
+            when_in(u - s, 0, NC)(lambda: ag_middle(u - s, s))
+
         at_pos(t, rs_send, first=1)
-        for s in (1, 2, 3):
-            at_pos(t - s, functools.partial(lambda s, c: rs_middle(c, s), s))
-        at_pos(t - 4, rs_final)
-        when_in(t - 3, 8, NC)(functools.partial(gelu, t - 3))
-        when_in(u, 0, NC)(functools.partial(ag_open, u))
-        for s in (1, 2, 3):
-            when_in(u - s, 0, NC)(functools.partial(ag_middle, u - s, s))
-
-        @pl.when(u == NC + 3)
-        def _():
-            ag_far(u - 4)
-            sum_open(1, far_p)
+        when_in(u, 0, NC)(lambda: ag_open(u))
+        middle(1)
+
+        @pl.when(t + 2 < NC)
+        def _():
+            w_forward(rs_id(t + 2))
+
+        when_in(u - 5, 0, NC - 2)(lambda: g_mid(u - 5))
+        middle(2)
 
         @pl.when(t == 0)
         def _():
             cot_pair(plus_p)
             cot_pair(minus_p)
-
-        @pl.when(t + 2 < NC)
-        def _():
-            w_forward(rs_id(t + 2))
 
         def sides(c):
             rs_pair(c, plus_p)
@@ -524,47 +522,59 @@
             cot_pair(own_p)
 
         at_pos(t - 1, lambda c: rs_pair(c, own_p))
+        when_in(u - 1, 0, NC)(lambda: ag_pair(u - 1, own_p))
+
+        @when_in(u - 4, 0, NC - 1)
+        def _():
+            ag_pair(u - 4, plus_p)
+            ag_pair(u - 4, minus_p)
+
+        middle(3)
         pl.when(t == 3)(stats_done)
 
         @pl.when(t + 2 < NC)
         def _():
             rs_far(t + 2)
+
+        when_in(u - 7, 0, NC - 4)(lambda: g_close(u - 7))
+        at_pos(t - 4, rs_final)
+        when_in(t - 3, 8, NC)(lambda: gelu(t - 3))
+        @when_in(u - 4, 0, NC - 1)
+        def _():
+            ag_far(u - 4)
+            g_open(u - 4)
 
         pl.when(t == 2)(stats_send)
         pl.when(t == 10)(attn_open)
         pl.when(t == 12)(attn_mid)
         pl.when(t == 15)(attn_close)
 
-        when_in(u - 4, 0, NC - 1)(functools.partial(ag_far, u - 4))
-
-        @when_in(u - 3, 0, NC)
-        def _():
-            ag_pair(u - 3, plus_p)
-            ag_pair(u - 3, minus_p)
-
-        when_in(u - 1, 0, NC)(functools.partial(ag_pair, u - 1, own_p))
-
-        when_in(u - 4, 0, NC)(functools.partial(g_open, u - 4))
-        when_in(u - 5, 0, NC - 1)(functools.partial(g_mid, u - 5))
-        when_in(u - 7, 0, NC - 3)(functools.partial(g_close, u - 7))
-
-        for j, a in ((0, 8), (1, NC - 1)):
-            pl.when(u == a + 1)(functools.partial(sum_open, j, own_p))
-
-            @pl.when(u == a + 3)
-            def _(j=j):
-                sum_open(j, plus_p)
-                sum_open(j, minus_p)
-                sum_mid(j, own_p)
-
-        pl.when(u == 12)(functools.partial(sum_open, 0, far_p))
-
-        @pl.when(u == 13)
-        def _():
-            sum_mid(0, plus_p)
-            sum_mid(0, minus_p)
-
-        pl.when(u == 14)(functools.partial(sum_mid, 0, far_p))
+        pl.when(u == 9)(lambda: sum_open(0, own_p))
+
+        @pl.when(u == 12)
+        def _():
+            sum_open(1, own_p)
+            sum_open(0, plus_p)
+            sum_open(0, minus_p)
+            sum_mid(0, own_p)
+            sum_open(0, far_p)
+
+        @pl.when(u == 14)
+        def _():
+            sum_mid(1, own_p)
+            for p in (plus_p, minus_p, far_p):
+                sum_mid(0, p)
+
+        @pl.when(u == 8)
+        def _():
+            for p in range(NP):
+                my_sent(0, p)
+
+        @when_in(u, 0, NC)
+        def _():
+            w_x(u).wait_send()
+            w_c(u).wait_send()
+            w_f(u).wait_send()
 
         for s in (4, 3, 2, 1):
 
@@ -573,12 +583,11 @@
                 ru(c, s - 1).wait_send()
 
             at_pos(t - s, sent)
-            a = u - s
-
-            @when_in(a, 0, NC)
-            def _(a=a, s=s):
-                ad(a, s - 1).wait_send()
-                au(a, s - 1).wait_send()
+
+            @when_in(u - s, 0, NC)
+            def _(s=s):
+                ad(u - s, s - 1).wait_send()
+                au(u - s, s - 1).wait_send()
 
         return 0
 
@@ -590,14 +599,18 @@
     def fy(k):
         return rcopy(fs_mid, fs_y.at[k - 1], fy_ss.at[k - 1], fy_rs.at[k - 1], at_my(lax.rem(my + k, 8)))
 
+    for p in (plus_p, minus_p):
+        ag_pair(NC - 1, p)
+        sum_open(1, p)
+    g_mid(NC - 2)
+    ag_far(NC - 1)
+    sum_open(1, far_p)
     for k in range(1, 8):
         fz(k).start()
+    g_open(NC - 1)
     sum_mid(1, plus_p)
     sum_mid(1, minus_p)
     g_mid(NC - 1)
-    out_copies = [pltpu.make_async_copy(gout.at[i], piece(i, gd, gu, gw, gq), wl_sem.at[i]) for i in range(NC)]
-    for i in range(NC - 3):
-        out_copies[i].start()
     for k in range(1, 8):
         fz(k).wait()
     tot = fs_own[...]
@@ -607,9 +620,14 @@
     for k in range(1, 8):
         fy(k).start()
     sum_mid(1, far_p)
+    out_copies = [pltpu.make_async_copy(gout.at[i], piece(i, gd, gu, gw, gq), wl_sem.at[i]) for i in range(NC)]
+    for i in range(NC - 4):
+        out_copies[i].start()
+    ad(NC - 1, 3).wait_send()
+    au(NC - 1, 3).wait_send()
     for p in range(NP):
         upd[p * PT : (p + 1) * PT, :] = jnp.transpose(sum_close(0, p), (1, 0)).astype(BF16)
-    for i in range(NC - 3, NC):
+    for i in range(NC - 4, NC):
         g_close(i)
         out_copies[i].start()
     for k in range(1, 8):
@@ -624,17 +642,6 @@
         tgr[p * PT : (p + 1) * PT, :] = jnp.transpose(st_tot[:, p * PT : (p + 1) * PT] * grad, (1, 0)).astype(BF16)
     for c in out_copies:
         c.wait()
-
-    for p in range(NP):
-        my_sent(0, p)
-
-    def w_done(i, _):
-        w_x(i).wait_send()
-        w_c(i).wait_send()
-        w_f(i).wait_send()
-        return 0
-
-    lax.fori_loop(0, NC, w_done, 0)
 
 
 def copy_kernel(*refs):

time: 156 us -> 152 us (0.974)
  Pallas kernels: 155 us -> 151 us
    pallas_call x1, Pallas kernels: 152 us -> 149 us  [fused(): pl.pallas_call(kernel, out_shape=(jax.ShapeDtypeStruct((TOK, FW), BF16),...]
where the time goes in v5:
time: 152 us
  Pallas kernels  151 us (99%)
    pallas_call x1, Pallas kernels, fused(): pl.pallas_call(kernel, out_shape=(jax.ShapeDtypeStruct((TOK, FW), BF16),...  149 us

profile of v5, /device:TPU:2, one launch (start us, length us, event | category | flops | bytes accessed | tf_op | source)
XLA Modules:
  0.0 151.9 jit_solution(7716924634664295372)
XLA Ops:
  0.6 148.8 %shard_map.109 = (bf16[512,96]{1,0:T(8,128)(2,1)}, bf16[512,96]{1,0:T(8,128)(2,1)}, bf16[192,1536]{1,0:T(8,128)(2,1)}, bf16[192,1536]{1,0:T(8,128)(2,1)}, bf16[1...) custom-call(bf16[512,96]{1,0:T(8,128)(2,1)} %bitcast.13, bf16[512,96]{1,0:T(8,128)(2,1)} %bitcast.14, ...), custom_call_target="tpu_custom_call" | custom-call | tf_op jit(solution)/shard_map/pallas_call | solution.py:731
  149.4 2.5 %shard_map.110 = (bf16[512,96]{1,0:T(8,128)(2,1)}, bf16[512,96]{1,0:T(8,128)(2,1)}, bf16[192,1536]{1,0:T(8,128)(2,1)}, bf16[192,1536]{1,0:T(8,128)(2,1)}, bf16[1...) custom-call(bf16[512,96]{1,0:T(8,128)(2,1)} %get-tuple-element.18.refs_0_, bf16[512,96]{1,0:T(8,128)(2,1)} %get-tuple-element.19.refs_1_, ...), custom_call_target="tpu_custom_call" | custom-call | tf_op jit(solution)/shard_map/pallas_call | solution.py:665

commit v6 on v5

--- a/solution.py
+++ b/solution.py
@@ -603,14 +603,16 @@
         ag_pair(NC - 1, p)
         sum_open(1, p)
     g_mid(NC - 2)
-    ag_far(NC - 1)
+    ad_wait(NC - 1, 3)
+    au_wait(NC - 1, 3)
+    g_open(NC - 1)
+    ag_pair(NC - 1, far_p)
     sum_open(1, far_p)
     for k in range(1, 8):
         fz(k).start()
-    g_open(NC - 1)
+    g_mid(NC - 1)
     sum_mid(1, plus_p)
     sum_mid(1, minus_p)
-    g_mid(NC - 1)
     for k in range(1, 8):
         fz(k).wait()
     tot = fs_own[...]

time: 152 us -> 150 us (0.987)
    pallas_call x1, Pallas kernels: 149 us -> 147 us  [fused(): pl.pallas_call(kernel, out_shape=(jax.ShapeDtypeStruct((TOK, FW), BF16),...]
where the time goes in v6:
time: 150 us
  Pallas kernels  150 us (100%)
    pallas_call x1, Pallas kernels, fused(): pl.pallas_call(kernel, out_shape=(jax.ShapeDtypeStruct((TOK, FW), BF16),...  147 us

profile of v6, /device:TPU:2, one launch (start us, length us, event | category | flops | bytes accessed | tf_op | source)
XLA Modules:
  0.0 150.3 jit_solution(1711934363557302761)
XLA Ops:
  0.6 147.2 %shard_map.109 = (bf16[512,96]{1,0:T(8,128)(2,1)}, bf16[512,96]{1,0:T(8,128)(2,1)}, bf16[192,1536]{1,0:T(8,128)(2,1)}, bf16[192,1536]{1,0:T(8,128)(2,1)}, bf16[1...) custom-call(bf16[512,96]{1,0:T(8,128)(2,1)} %bitcast.13, bf16[512,96]{1,0:T(8,128)(2,1)} %bitcast.14, ...), custom_call_target="tpu_custom_call" | custom-call | tf_op jit(solution)/shard_map/pallas_call | solution.py:733
  147.8 2.5 %shard_map.110 = (bf16[512,96]{1,0:T(8,128)(2,1)}, bf16[512,96]{1,0:T(8,128)(2,1)}, bf16[192,1536]{1,0:T(8,128)(2,1)}, bf16[192,1536]{1,0:T(8,128)(2,1)}, bf16[1...) custom-call(bf16[512,96]{1,0:T(8,128)(2,1)} %get-tuple-element.18.refs_0_, bf16[512,96]{1,0:T(8,128)(2,1)} %get-tuple-element.19.refs_1_, ...), custom_call_target="tpu_custom_call" | custom-call | tf_op jit(solution)/shard_map/pallas_call | solution.py:667

commit v7 on v6

--- a/solution.py
+++ b/solution.py
@@ -613,6 +613,12 @@
     g_mid(NC - 1)
     sum_mid(1, plus_p)
     sum_mid(1, minus_p)
+    out_copies = [pltpu.make_async_copy(gout.at[i], piece(i, gd, gu, gw, gq), wl_sem.at[i]) for i in range(NC)]
+    g_close(NC - 4)
+    for i in range(NC - 3):
+        out_copies[i].start()
+    for p in range(NP):
+        upd[p * PT : (p + 1) * PT, :] = jnp.transpose(sum_close(0, p), (1, 0)).astype(BF16)
     for k in range(1, 8):
         fz(k).wait()
     tot = fs_own[...]
@@ -622,14 +628,9 @@
     for k in range(1, 8):
         fy(k).start()
     sum_mid(1, far_p)
-    out_copies = [pltpu.make_async_copy(gout.at[i], piece(i, gd, gu, gw, gq), wl_sem.at[i]) for i in range(NC)]
-    for i in range(NC - 4):
-        out_copies[i].start()
     ad(NC - 1, 3).wait_send()
     au(NC - 1, 3).wait_send()
-    for p in range(NP):
-        upd[p * PT : (p + 1) * PT, :] = jnp.transpose(sum_close(0, p), (1, 0)).astype(BF16)
-    for i in range(NC - 4, NC):
+    for i in range(NC - 3, NC):
         g_close(i)
         out_copies[i].start()
     for k in range(1, 8):

time: 150 us -> 151 us (level)
  no operation moved by 1% of the time
where the time goes in v7:
time: 151 us
  Pallas kernels  150 us (99%)
    pallas_call x1, Pallas kernels, fused(): pl.pallas_call(kernel, out_shape=(jax.ShapeDtypeStruct((TOK, FW), BF16),...  147 us

profile of v7, /device:TPU:2, one launch (start us, length us, event | category | flops | bytes accessed | tf_op | source)
XLA Modules:
  0.0 150.6 jit_solution(16823131528199720683)
XLA Ops:
  0.6 147.5 %shard_map.109 = (bf16[512,96]{1,0:T(8,128)(2,1)}, bf16[512,96]{1,0:T(8,128)(2,1)}, bf16[192,1536]{1,0:T(8,128)(2,1)}, bf16[192,1536]{1,0:T(8,128)(2,1)}, bf16[1...) custom-call(bf16[512,96]{1,0:T(8,128)(2,1)} %bitcast.13, bf16[512,96]{1,0:T(8,128)(2,1)} %bitcast.14, ...), custom_call_target="tpu_custom_call" | custom-call | tf_op jit(solution)/shard_map/pallas_call | solution.py:734
  148.1 2.5 %shard_map.110 = (bf16[512,96]{1,0:T(8,128)(2,1)}, bf16[512,96]{1,0:T(8,128)(2,1)}, bf16[192,1536]{1,0:T(8,128)(2,1)}, bf16[192,1536]{1,0:T(8,128)(2,1)}, bf16[1...) custom-call(bf16[512,96]{1,0:T(8,128)(2,1)} %get-tuple-element.18.refs_0_, bf16[512,96]{1,0:T(8,128)(2,1)} %get-tuple-element.19.refs_1_, ...), custom_call_target="tpu_custom_call" | custom-call | tf_op jit(solution)/shard_map/pallas_call | solution.py:668
